TPU v7x, 32 devices: a whole 2x2x4 slice. The times are simulated.
32 devices in a mesh: curve: 8 (over z, y), sub: 4 (over x, core).
Axes of the slice: x: 2, y: 2, z: 4, core: 2. Of those that a mesh axis runs over, the one named last changes fastest.
Arguments:
- densities: bfloat16 [192, 16384], P(None, ('curve', 'sub')), may hold values from -6 to 6
- far_lists: int32 [200, 16384], P(None, ('curve', 'sub')), may hold values from 0 to 1536
- near_lists: int32 [26, 16384], P(None, ('curve', 'sub')), may hold values from 0 to 1535
- ghost_sends: int32 [32768], P(('curve', 'sub')), may hold values from 0 to 511
- top_lists: int32 [200, 32], P(None, ('curve', 'sub')), may hold values from 0 to 32
- point_to_mult: bfloat16 [32256], replicated, may hold values from -0.4375 to 0.4375
- mult_to_mult: bfloat16 [225792], replicated, may hold values from -0.15625 to 0.15625
- mult_to_local: bfloat16 [5644800], replicated, may hold values from -0.03125 to 0.03125
- local_to_local: bfloat16 [225792], replicated, may hold values from -0.5 to 0.5
- local_to_point: bfloat16 [32256], replicated, may hold values from -0.5 to 0.5
- point_to_point: bfloat16 [995328], replicated, may hold values from -0.078125 to 0.078125
Outputs:
- velocity: float32 [192, 16384], P(None, ('curve', 'sub'))
Inputs may be any that keep to these rules, and one draw needn't show every extreme that they name: `far_lists`: an entry equal to 1536 marks an absent interaction. `ghost_sends`: entries are leaf indices local to the sending device. `top_lists`: an entry equal to 32 marks an absent interaction.
All inputs are finite; a program needn't handle non-finite values.
Results may differ from a plain program's by a relative error of at most 0.0085.
Values may be sent and summed in bfloat16 or wider, within the bound.
A program may use at most 192 MiB of HBM per device.

v0:
```python
import jax
import jax.numpy as jnp
from jax import lax
from jax.sharding import PartitionSpec as P

LEVELS = 3


def shards(
    densities,
    far_lists,
    near_lists,
    ghost_sends,
    top_lists,
    point_to_mult,
    mult_to_mult,
    mult_to_local,
    local_to_local,
    local_to_point,
    point_to_point,
):
    dwidth, leaf_count = densities.shape
    offset_count = far_lists.shape[0]
    near_count = near_lists.shape[0]
    ewidth = point_to_mult.shape[0] // dwidth
    p2m = point_to_mult.reshape(dwidth, ewidth)
    m2m = mult_to_mult.reshape(8, ewidth, ewidth)
    m2l = mult_to_local.reshape(offset_count, ewidth, ewidth)
    l2l = local_to_local.reshape(8, ewidth, ewidth)
    l2p = local_to_point.reshape(ewidth, dwidth)
    p2p = point_to_point.reshape(near_count + 1, dwidth, dwidth)
    dens_rows = densities.T
    mult_rows = jnp.einsum("dl,de->le", densities, p2m, preferred_element_type=jnp.float32).astype(
        jnp.bfloat16
    )
    level_mult = mult_rows.T
    for level_index in range(LEVELS):
        grouped = level_mult.reshape(ewidth, -1, 8)
        level_mult = jnp.einsum(
            "ebk,kef->fb", grouped, m2m, preferred_element_type=jnp.float32
        ).astype(jnp.bfloat16)
    packed = dens_rows[ghost_sends]
    arrived = lax.all_to_all(packed, ("curve", "sub"), split_axis=0, concat_axis=0, tiled=True)
    arrived_mult = jnp.einsum("ld,de->le", arrived, p2m, preferred_element_type=jnp.float32).astype(
        jnp.bfloat16
    )
    top_boxes = lax.all_gather(level_mult.T, ("curve", "sub"), axis=0, tiled=True)
    top_pool = jnp.concatenate([top_boxes, jnp.zeros((1, ewidth), jnp.bfloat16)], axis=0)
    picked = top_pool[top_lists]
    local_exp = jnp.einsum("cbe,cef->fb", picked, m2l, preferred_element_type=jnp.float32).astype(
        jnp.bfloat16
    )
    leaf_far = None
    for level_index in range(LEVELS):
        child_exp = jnp.einsum(
            "eb,kef->fbk", local_exp, l2l, preferred_element_type=jnp.float32
        ).reshape(ewidth, -1)
        if level_index < LEVELS - 1:
            local_exp = child_exp.astype(jnp.bfloat16)
        else:
            leaf_far = child_exp
    mult_pool = jnp.concatenate(
        [mult_rows, arrived_mult, jnp.zeros((1, ewidth), jnp.bfloat16)], axis=0
    )
    gathered = mult_pool[far_lists]
    leaf_local = (
        leaf_far + jnp.einsum("cle,cef->fl", gathered, m2l, preferred_element_type=jnp.float32)
    ).astype(jnp.bfloat16)
    far_vel = jnp.einsum("el,ed->dl", leaf_local, l2p, preferred_element_type=jnp.float32)
    dens_pool = jnp.concatenate([dens_rows, arrived], axis=0)
    neighbours = dens_pool[near_lists]
    near_vel = jnp.einsum(
        "cld,cdf->fl", neighbours, p2p[:near_count], preferred_element_type=jnp.float32
    )
    self_vel = jnp.einsum(
        "dl,df->fl", densities, p2p[near_count], preferred_element_type=jnp.float32
    )
    return far_vel + near_vel + self_vel


def solution(mesh):
    in_specs = (
        P(None, ("curve", "sub")),
        P(None, ("curve", "sub")),
        P(None, ("curve", "sub")),
        P(("curve", "sub")),
        P(None, ("curve", "sub")),
        P(),
        P(),
        P(),
        P(),
        P(),
        P(),
    )
    out_specs = P(None, ("curve", "sub"))
    return jax.shard_map(shards, mesh=mesh, in_specs=in_specs, out_specs=out_specs, check_vma=False)
```

profile of v0, /device:TPU:0, one launch (start us, length us, event | category | flops | bytes accessed | tf_op | source)
XLA Modules:
  0.0 627.6 jit_solution(13082657046908637117)
XLA Ops:
  0.0 1.1 copy.20
  1.1 0.7 fusion.19
  1.8 5.0 gather_fusion.1
  6.8 7.3 %all-to-all-start = ((bf16[32,32,192]{2,1,0:T(8,128)(2,1)}), bf16[32,32,192]{2,1,0:T(8,128)(2,1)S(1)}, u32[]{:S(2)}, u32[]{:S(2)}) async-start(bf16[32,32,192]{2,1,0:T(8,128)(2,1)} %bitcast.23), calls=%async_computation | async-start | bytes 1048576 | tf_op jit(solution)/shard_map/all_to_all | solution.py:43
  14.1 1.1 reshape.65
  15.2 1.2 convolution_convert_fusion.1
  16.6 0.8 broadcast_clamp_fusion
  17.4 52.9 %reshape.70 = bf16[200,168,168]{2,1,0:T(8,128)(2,1)} reshape(bf16[5644800]{0:T(1024)(128)(2,1)} %param.18) | data formatting | bytes 22579200 | tf_op jit(solution)/shard_map/reshape | solution.py:28
  70.4 2.0 reshape.71
  72.4 2.0 reshape.67
  74.5 0.3 fusion.5
  75.0 0.3 fusion.15
  75.3 0.3 dynamic-update-slice
  75.5 40.9 %all-reduce.1 = bf16[5376]{0:T(1024)(128)(2,1)S(1)} all-reduce(bf16[5376]{0:T(1024)(128)(2,1)S(1)} %dynamic-update-slice), channel_id=2, replica_groups=mesh['curve'=8,'sub'=4] {'curve','sub'}, use_global_device_ids=true, to_apply=%add.1 | all-reduce | flops 5376 | bytes 21504
  116.6 1.0 gather_fusion
  117.6 8.4 %fusion.10 = f32[1,168,1]{1,0,2:T(1,128)S(1)} fusion(bf16[200,168,168]{2,1,0:T(8,128)(2,1)} %reshape.70, bf16[200,168,1]{1,0,2:T(8,128)(2,1)S(1)} %bitcast.100), kind=kOutput, calls=%fused_computation.28 | convolution fusion | flops 11289600 | bytes 11357472 | tf_op jit(solution)/shard_map/cbe,cef->fb/dot_general | solution.py:50
  126.2 0.8 fusion.4
  127.1 0.6 reshape.100
  127.7 2.9 slice.27
  130.7 1.6 reshape.73
  132.3 0.7 squeeze.3
  133.0 1.8 convolution_bitcast_fusion
  134.8 0.8 broadcast_clamp_fusion.1
  135.8 1.2 convolution_convert_fusion
  137.0 1.0 maximum_maximum_fusion
  138.0 0.3 copy.21
  138.3 53.1 %gather_fusion.3 = bf16[13312,192]{1,0:T(8,128)(2,1)} fusion(bf16[1536,192]{1,0:T(8,128)(2,1)S(1)} %pad_maximum_fusion, s32[13312]{0:T(1024)S(1)} %broadcast_clamp_fusion.1), kind=kCustom, calls=%fused_computation.3 | custom fusion | bytes 10276864 | tf_op jit(solution)/shard_map/gather | solution.py:71
  191.5 6.9 %convolution_bitcast_fusion.2 = f32[512,192]{0,1:T(8,128)} fusion(bf16[26,512,192]{2,1,0:T(8,128)(2,1)} %bitcast.95, bf16[26,192,192]{2,1,0:T(8,128)(2,1)} %slice.27), kind=kOutput, calls=%fused_computation.9 | convolution fusion | flops 981467136 | bytes 7421952 | tf_op jit(solution)/shard_map/cld,cdf->fl/dot_general | solution.py:72
  198.4 402.2 %gather_fusion.2 = bf16[102400,168]{1,0:T(8,128)(2,1)} fusion(bf16[1537,168]{1,0:T(8,128)(2,1)S(1)} %copy.21, s32[102400]{0:T(1024)S(1)} %copy-done.1), kind=kCustom, calls=%fused_computation.2 | custom fusion | bytes 69222400 | tf_op jit(solution)/shard_map/gather | solution.py:65
  600.6 25.6 %fusion.2 = bf16[168,512]{0,1:T(8,128)(2,1)S(1)} fusion(bf16[200,512,168]{2,1,0:T(8,128)(2,1)} %bitcast.94, bf16[200,168,168]{2,1,0:T(8,128)(2,1)} %reshape.70, f32[168,64,8]{0,1,2:T(8,128)S(1)} %copy-done.5), kind=kOutput, calls=%fused_computation.13 | convolution fusion | flops 5780447232 | bytes 46212096 | tf_op jit(solution)/shard_map/cle,cef->fl/dot_general | solution.py:67
  626.3 0.3 fusion.1
  626.6 1.0 convolution_add_fusion
  (47 shorter events, 1.1 us)
Async XLA Ops:
  0.0 16.4 %copy-start.8 = (s32[200,512]{1,0:T(8,128)S(1)}, s32[200,512]{1,0:T(8,128)}, u32[]{:S(2)}) copy-start(s32[200,512]{1,0:T(8,128)} %param.12) | copy-start | bytes 1228804
  6.8 128.9 %all-to-all-start = ((bf16[32,32,192]{2,1,0:T(8,128)(2,1)}), bf16[32,32,192]{2,1,0:T(8,128)(2,1)S(1)}, u32[]{:S(2)}, u32[]{:S(2)}) async-start(bf16[32,32,192]{2,1,0:T(8,128)(2,1)} %bitcast.23), calls=%async_computation | async-start | bytes 1048576 | tf_op jit(solution)/shard_map/all_to_all | solution.py:43
  15.2 55.1 %copy-start.4 = (bf16[192,168]{1,0:T(8,128)(2,1)}, bf16[192,168]{1,0:T(8,128)(2,1)S(1)}, u32[]{:S(2)}) copy-start(bf16[192,168]{1,0:T(8,128)(2,1)S(1)} %reshape.65) | copy-start | bytes 193540
  16.5 57.9 %copy-start.3 = (bf16[512,168]{0,1:T(8,128)(2,1)}, bf16[512,168]{0,1:T(8,128)(2,1)S(1)}, u32[]{:S(2)}) copy-start(bf16[512,168]{0,1:T(8,128)(2,1)S(1)} %convolution_convert_fusion.1) | copy-start | bytes 516100
  17.4 52.9 %copy-start.6 = (bf16[225792]{0:T(1024)(128)(2,1)S(1)}, bf16[225792]{0:T(1024)(128)(2,1)}, u32[]{:S(2)}) copy-start(bf16[225792]{0:T(1024)(128)(2,1)} %param.19) | copy-start | bytes 1354756
  17.4 54.9 %copy-start.7 = (bf16[225792]{0:T(1024)(128)(2,1)S(1)}, bf16[225792]{0:T(1024)(128)(2,1)}, u32[]{:S(2)}) copy-start(bf16[225792]{0:T(1024)(128)(2,1)} %param.17) | copy-start | bytes 1354756
  17.4 99.1 %copy-start.12 = (s32[200,1]{0,1:T(1,128)S(1)}, s32[200,1]{0,1:T(1,128)}, u32[]{:S(2)}) copy-start(s32[200,1]{0,1:T(1,128)} %param.15) | copy-start | bytes 2404
  117.6 9.5 %copy-start.11 = (s32[26,512]{1,0:T(8,128)S(1)}, s32[26,512]{1,0:T(8,128)}, u32[]{:S(2)}) copy-start(s32[26,512]{1,0:T(8,128)} %param.13) | copy-start | bytes 159748
  126.0 1.7 slice-start
  126.0 6.3 slice-start.1
  191.5 6.9 %copy-start.1 = (s32[102400]{0:T(1024)S(1)}, s32[102400]{0:T(1024)}, u32[]{:S(2)}) copy-start(s32[102400]{0:T(1024)} %broadcast_clamp_fusion) | copy-start | bytes 1228804
  198.4 402.2 %copy-start.5 = (f32[168,64,8]{0,1,2:T(8,128)S(1)}, f32[168,64,8]{0,1,2:T(8,128)}, u32[]{:S(2)}) copy-start(f32[168,64,8]{0,1,2:T(8,128)} %convolution_bitcast_fusion) | copy-start | bytes 1032196
  600.6 25.7 %copy-start.2 = (f32[512,192]{0,1:T(8,128)S(1)}, f32[512,192]{0,1:T(8,128)}, u32[]{:S(2)}) copy-start(f32[512,192]{0,1:T(8,128)} %convolution_bitcast_fusion.2) | copy-start | bytes 1179652
  600.6 25.7 %copy-start.10 = (bf16[168,192]{1,0:T(8,128)(2,1)S(1)}, bf16[168,192]{1,0:T(8,128)(2,1)}, u32[]{:S(2)}) copy-start(bf16[168,192]{1,0:T(8,128)(2,1)} %reshape.73) | copy-start | bytes 193540
  600.6 26.0 %copy-start = (bf16[192,512]{1,0:T(8,128)(2,1)S(1)}, bf16[192,512]{1,0:T(8,128)(2,1)}, u32[]{:S(2)}) copy-start(bf16[192,512]{1,0:T(8,128)(2,1)} %param.11) | copy-start | bytes 589828
  600.6 26.0 %copy-start.9 = (bf16[192,192]{1,0:T(8,128)(2,1)S(1)}, bf16[192,192]{1,0:T(8,128)(2,1)}, u32[]{:S(2)}) copy-start(bf16[192,192]{1,0:T(8,128)(2,1)} %squeeze.3) | copy-start | bytes 221188
where the time goes:
time: 628 us
  local copies, waits for them, and re-layouts  527 us (84%)
  matrix products  48.2 us (8%)
  blocking collectives  40.9 us (7%)
  starting transfers between devices  7.3 us (1%)
    gather x1, local copies, waits for them, and re-layouts, shards(): gathered = mult_pool[far_lists]  402 us
    gather x1, local copies, waits for them, and re-layouts, shards(): neighbours = dens_pool[near_lists]  53.1 us
    reshape x1, local copies, waits for them, and re-layouts, shards(): m2l = mult_to_local.reshape(offset_count, ewidth, ewidth)  52.9 us
    unnamed x1, blocking collectives  40.9 us
    dot_general x1, matrix products, shards(): jnp.einsum('cle,cef->fl', gathered, m2l, preferred_element_type=jnp.float32)  25.6 us
  transfers between devices with their start and end apart: 1, of which 0 were waited for; matrix products, arithmetic and copies ran while one was open for 13% of the time, Pallas kernels for 0%

commit v1 on v0

v1 whole, which is shorter than its diff:
```python
import jax
import jax.numpy as jnp
from jax import lax
from jax.experimental import pallas as pl
from jax.experimental.pallas import tpu as pltpu
from jax.sharding import PartitionSpec as P

LEVELS = 3
BLOCK = 8
BF = jnp.bfloat16
F32 = jnp.float32


def one_hot(row, depth):
    shape = (depth, row.shape[1])
    key = jnp.broadcast_to(row.astype(jnp.int16), shape)
    ids = lax.broadcasted_iota(jnp.int16, shape, 0)
    return jnp.where(key == ids, jnp.ones(shape, BF), jnp.zeros(shape, BF))


def dot_t(left, right):
    return lax.dot_general(left, right, (((0,), (0,)), ((), ())), preferred_element_type=F32)


def far_kernel(lists, m2l, pool, top, far, top_far, picked):
    ewidth, depth = pool.shape

    @pl.when(pl.program_id(0) == 0)
    def _():
        far[...] = jnp.zeros_like(far)
        top_far[...] = jnp.zeros_like(top_far)

    @pl.loop(0, BLOCK // 2)
    def _(pair):
        both = []
        for half in range(2):
            hot = one_hot(lists[pl.ds(2 * pair + half, 1), :], depth)
            both.append(jnp.dot(pool[...], hot, preferred_element_type=F32))
        start = pl.multiple_of(pair * (2 * ewidth), 16)
        picked[pl.ds(start, 2 * ewidth), :] = jnp.concatenate(both, axis=0).astype(BF)

    far[...] += dot_t(m2l[...], picked[...])
    top_far[...] += jnp.dot(top[0], m2l[...], preferred_element_type=F32)


def far_call(far_lists, m2l_rows, pool, top):
    offsets, leaves = far_lists.shape
    ewidth, depth = pool.shape
    rows = BLOCK * ewidth
    return pl.pallas_call(
        far_kernel,
        grid=(offsets // BLOCK,),
        in_specs=[
            pl.BlockSpec((BLOCK, leaves), lambda i: (i, 0)),
            pl.BlockSpec((rows, ewidth), lambda i: (i, 0)),
            pl.BlockSpec((ewidth, depth), lambda i: (0, 0)),
            pl.BlockSpec((1, 1, rows), lambda i: (i, 0, 0)),
        ],
        out_specs=[
            pl.BlockSpec((ewidth, leaves), lambda i: (0, 0)),
            pl.BlockSpec((1, ewidth), lambda i: (0, 0)),
        ],
        out_shape=[
            jax.ShapeDtypeStruct((ewidth, leaves), F32),
            jax.ShapeDtypeStruct((1, ewidth), F32),
        ],
        scratch_shapes=[pltpu.VMEM((rows, leaves), BF)],
        compiler_params=pltpu.CompilerParams(vmem_limit_bytes=48 * 2**20),
    )(far_lists, m2l_rows, pool, top)


def near_kernel(lists, p2p, pool, out, picked):
    dwidth, depth = pool.shape
    classes, leaves = lists.shape

    @pl.loop(0, classes)
    def _(c):
        hot = one_hot(lists[pl.ds(c, 1), :], depth)
        found = jnp.dot(pool[...], hot, preferred_element_type=F32).astype(BF)
        picked[pl.ds(pl.multiple_of(c * dwidth, 16), dwidth), :] = found

    picked[classes * dwidth :, :] = pool[:, :leaves]
    out[...] = dot_t(p2p[...], picked[...])


def near_call(near_lists, p2p_rows, pool):
    classes, leaves = near_lists.shape
    dwidth, depth = pool.shape
    return pl.pallas_call(
        near_kernel,
        out_shape=jax.ShapeDtypeStruct((dwidth, leaves), F32),
        scratch_shapes=[pltpu.VMEM(((classes + 1) * dwidth, leaves), BF)],
        compiler_params=pltpu.CompilerParams(vmem_limit_bytes=48 * 2**20),
    )(near_lists, p2p_rows, pool)


def shards(
    densities,
    far_lists,
    near_lists,
    ghost_sends,
    top_lists,
    point_to_mult,
    mult_to_mult,
    mult_to_local,
    local_to_local,
    local_to_point,
    point_to_point,
):
    axes = ("curve", "sub")
    devices = lax.axis_size(axes)
    dwidth, leaf_count = densities.shape
    offset_count = far_lists.shape[0]
    near_count = near_lists.shape[0]
    ewidth = point_to_mult.shape[0] // dwidth
    p2m = point_to_mult.reshape(dwidth, ewidth)
    m2m = mult_to_mult.reshape(8, ewidth, ewidth)
    m2l_rows = mult_to_local.reshape(offset_count * ewidth, ewidth)
    l2l = local_to_local.reshape(8, ewidth, ewidth)
    l2p = local_to_point.reshape(ewidth, dwidth)
    p2p_rows = point_to_point.reshape((near_count + 1) * dwidth, dwidth)

    sends = ghost_sends[:, None] == lax.broadcasted_iota(jnp.int32, (1, leaf_count), 1)
    packed = lax.dot_general(
        sends.astype(BF), densities, (((1,), (1,)), ((), ())), preferred_element_type=F32
    ).astype(BF)
    arrived = lax.all_to_all(packed, axes, split_axis=0, concat_axis=0, tiled=True)

    mult_rows = jnp.einsum("dl,de->le", densities, p2m, preferred_element_type=F32).astype(BF)
    level_mult = mult_rows.T
    for level_index in range(LEVELS):
        grouped = level_mult.reshape(ewidth, -1, 8)
        level_mult = jnp.einsum("ebk,kef->fb", grouped, m2m, preferred_element_type=F32).astype(BF)
    mine = level_mult.T
    copies = jnp.broadcast_to(mine[None], (devices,) + mine.shape)
    top_boxes = lax.all_to_all(copies, axes, split_axis=0, concat_axis=0, tiled=True)
    top_boxes = top_boxes.reshape(-1, ewidth)
    top_hot = top_lists == lax.broadcasted_iota(jnp.int32, (1, top_boxes.shape[0]), 1)
    top_picked = jnp.dot(top_hot.astype(BF), top_boxes, preferred_element_type=F32).astype(BF)

    dens_pool = jnp.concatenate([densities, arrived.T], axis=1)
    mult_pool = jnp.einsum("dl,de->el", dens_pool, p2m, preferred_element_type=F32).astype(BF)
    far, top_far = far_call(
        far_lists,
        m2l_rows,
        mult_pool,
        top_picked.reshape(offset_count // BLOCK, 1, BLOCK * ewidth),
    )
    near = near_call(near_lists, p2p_rows, dens_pool)

    local_exp = top_far.T.astype(BF)
    leaf_far = None
    for level_index in range(LEVELS):
        child_exp = jnp.einsum(
            "eb,kef->fbk", local_exp, l2l, preferred_element_type=F32
        ).reshape(ewidth, -1)
        if level_index < LEVELS - 1:
            local_exp = child_exp.astype(BF)
        else:
            leaf_far = child_exp
    leaf_local = (leaf_far + far).astype(BF)
    return near + jnp.einsum("el,ed->dl", leaf_local, l2p, preferred_element_type=F32)


def solution(mesh):
    in_specs = (
        P(None, ("curve", "sub")),
        P(None, ("curve", "sub")),
        P(None, ("curve", "sub")),
        P(("curve", "sub")),
        P(None, ("curve", "sub")),
        P(),
        P(),
        P(),
        P(),
        P(),
        P(),
    )
    out_specs = P(None, ("curve", "sub"))
    return jax.shard_map(shards, mesh=mesh, in_specs=in_specs, out_specs=out_specs, check_vma=False)
```

time: 628 us -> 199 us (0.32)
  local copies, waits for them, and re-layouts: 527 us -> 73.3 us
  Pallas kernels: 0 us -> 102 us
  matrix products: 48.2 us -> 6 us
  blocking collectives: 40.9 us -> 0 us
    gather x4 -> x0, local copies, waits for them, and re-layouts: 461 us -> none  [the longest x1 402 us: shards(): gathered = mult_pool[far_lists]]
    pallas_call x0 -> x2, Pallas kernels: none -> 102 us  [the longest x1 88.3 us: far_call(): pl.pallas_call(far_kernel, grid=(offsets // BLOCK,), in_specs=[pl.BlockSp...]
    dot_general x13 -> x11, matrix products: 48.2 us -> 6 us  [the longest x1 1.45 us: shards(): jnp.einsum('dl,de->el', dens_pool, p2m, preferred_element_type=F32)]
    unnamed x1 -> x0, blocking collectives: 40.9 us -> none
    reshape x1 -> x4, local copies, waits for them, and re-layouts: 52.9 us -> 59.1 us  [the longest x1 52.9 us: shards(): m2l_rows = mult_to_local.reshape(offset_count * ewidth, ewidth)]
  transfers between devices with their start and end apart: 1 -> 2, of which waited for: 0 -> 1; matrix products, arithmetic and copies ran while one was open for 13% -> 32% of each run, Pallas kernels for 0% -> 0%
where the time goes in v1:
time: 199 us; the launch traced here: 198 us
  Pallas kernels  102 us (51%)
  local copies, waits for them, and re-layouts  73.3 us (37%)
  starting transfers between devices  9.9 us (5%)
  matrix products  6 us (3%)
  waiting for transfers between devices  5.52 us (3%)
    pallas_call x1, Pallas kernels, far_call(): pl.pallas_call(far_kernel, grid=(offsets // BLOCK,), in_specs=[pl.BlockSp...  88.3 us
    reshape x1, local copies, waits for them, and re-layouts, shards(): m2l_rows = mult_to_local.reshape(offset_count * ewidth, ewidth)  52.9 us
    pallas_call x1, Pallas kernels, near_call(): pl.pallas_call(near_kernel, out_shape=jax.ShapeDtypeStruct((dwidth, leave...  14.1 us
    all_to_all x1, starting transfers between devices, shards(): lax.all_to_all(copies, axes, split_axis=0, concat_axis=0, tiled=True)  7.3 us
    all_to_all x1, waiting for transfers between devices, shards(): lax.all_to_all(copies, axes, split_axis=0, concat_axis=0, tiled=True)  5.52 us
    reshape x1, local copies, waits for them, and re-layouts, shards(): p2p_rows = point_to_point.reshape((near_count + 1) * dwidth, dwidth)  4.01 us
  transfers between devices with their start and end apart: 2, of which 1 were waited for; matrix products, arithmetic and copies ran while one was open for 32% of the time, Pallas kernels for 0%

profile of v1, /device:TPU:0, one launch (start us, length us, event | category | flops | bytes accessed | tf_op | source)
XLA Modules:
  0.0 198.5 jit_solution(9642472167632754808)
XLA Ops:
  0.0 3.1 %reshape.61 = bf16[8,168,168]{2,1,0:T(8,128)(2,1)S(1)} reshape(bf16[225792]{0:T(1024)(128)(2,1)} %param.17) | data formatting | bytes 903168 | tf_op jit(solution)/shard_map/reshape | solution.py:117
  3.1 1.2 reshape.59
  4.3 0.6 copy-done.8
  4.9 1.1 convolution_convert_fusion.1
  6.2 0.3 fusion.6
  6.5 0.2 fusion.8
  6.7 0.3 fusion.17
  7.0 0.7 broadcast_in_dim.2
  7.7 7.3 %all-to-all-start.1 = ((bf16[32,1,168]{2,1,0:T(2,128)(2,1)}), bf16[32,1,168]{2,1,0:T(2,128)(2,1)S(1)}, u32[]{:S(2)}, u32[]{:S(2)}) async-start(bf16[32,1,168]{2,1,0:T(2,128)(2,1)} %broadcast_in_dim.2), calls=%async_computation.1 | async-start | bytes 65536 | tf_op jit(solution)/shard_map/all_to_all | solution.py:136
  15.0 0.7 fusion.2
  15.7 1.0 copy.24
  16.7 5.5 %all-to-all-done.1 = bf16[32,1,168]{2,1,0:T(2,128)(2,1)S(1)} async-done(((bf16[32,1,168]{2,1,0:T(2,128)(2,1)}), bf16[32,1,168]{2,1,0:T(2,128)(2,1)S(1)}, u32[]{:S(2)}, u32[]{:S(2)}) %all-to-all-start.1) | async-done | bytes 10784 | tf_op jit(solution)/shard_map/all_to_all | solution.py:136
  22.2 2.6 %all-to-all-start = ((bf16[32,32,192]{2,1,0:T(8,128)(2,1)}), bf16[32,32,192]{2,1,0:T(8,128)(2,1)S(1)}, u32[]{:S(2)}, u32[]{:S(2)}) async-start(bf16[32,32,192]{2,1,0:T(8,128)(2,1)} %bitcast), calls=%async_computation | async-start | bytes 1048576 | tf_op jit(solution)/shard_map/all_to_all | solution.py:127
  24.9 52.9 %reshape.58.m2l = bf16[33600,168]{1,0:T(8,128)(2,1)} reshape(bf16[5644800]{0:T(1024)(128)(2,1)} %param.18) | data formatting | bytes 22579200 | tf_op jit(solution)/shard_map/reshape | solution.py:118
  77.7 2.8 %reshape.65 = bf16[8,168,168]{2,1,0:T(8,128)(2,1)} reshape(bf16[225792]{0:T(1024)(128)(2,1)S(1)} %copy-done.7) | data formatting | bytes 903168 | tf_op jit(solution)/shard_map/reshape | solution.py:119
  80.6 4.0 %reshape.57.p2p = bf16[5184,192]{1,0:T(8,128)(2,1)S(1)} reshape(bf16[995328]{0:T(1024)(128)(2,1)} %param.21) | data formatting | bytes 3981312 | tf_op jit(solution)/shard_map/reshape | solution.py:121
  84.6 0.7 reshape.67
  85.3 0.3 convolution_convert_fusion.2
  85.7 0.3 reshape.76.top
  86.0 0.9 copy.25
  86.9 1.5 fusion.pool
  88.4 1.1 pad_maximum_fusion.pool
  89.5 1.0 copy-done
  90.5 88.3 %shard_map.110 = (f32[168,512]{1,0:T(8,128)S(1)}, f32[1,168]{1,0:T(1,128)S(1)}) custom-call(s32[200,512]{1,0:T(8,128)S(1)} %copy-done, bf16[33600,168]{1,0:T(8,128)(2,1)} %reshape.58.m2l, bf16[168,1536]{1,0:T(8,128)(2,1)S(1)} %fusion.pool, bf16[25,1,1344]{2,1,0:T(2,128)(2,1)S(1)} %reshape.76.top), custom_call_target="tpu_custom_call" | custom-call | tf_op jit(solution)/shard_map/pallas_call | solution.py:50
  178.9 0.7 copy-done.1
  179.6 0.2 fusion.21
  179.8 0.2 fusion.5
  180.0 0.3 convolution_bitcast_fusion
  180.3 1.1 copy.56
  181.4 1.9 copy.33
  183.3 14.1 %shard_map.109 = f32[192,512]{1,0:T(8,128)S(1)} custom-call(s32[26,512]{1,0:T(8,128)S(1)} %copy-done.3, bf16[5184,192]{1,0:T(8,128)(2,1)S(1)} %reshape.57.p2p, bf16[192,1536]{1,0:T(8,128)(2,1)S(1)} %pad_maximum_fusion.pool), custom_call_target="tpu_custom_call" | custom-call | tf_op jit(solution)/shard_map/pallas_call | solution.py:89
  197.5 1.0 fusion.3
  (27 shorter events, 0.3 us)
Async XLA Ops:
  3.1 11.9 %copy-start.6 = (bf16[192,512]{1,0:T(8,128)(2,1)S(1)}, bf16[192,512]{1,0:T(8,128)(2,1)}, u32[]{:S(2)}) copy-start(bf16[192,512]{1,0:T(8,128)(2,1)} %param.11) | copy-start | bytes 589828
  3.1 11.9 %copy-start.12 = (s32[1024]{0:T(1024)S(1)}, s32[1024]{0:T(1024)}, u32[]{:S(2)}) copy-start(s32[1024]{0:T(1024)} %param.14) | copy-start | bytes 12292
  4.3 0.6 copy-start.8
  7.7 14.6 %all-to-all-start.1 = ((bf16[32,1,168]{2,1,0:T(2,128)(2,1)}), bf16[32,1,168]{2,1,0:T(2,128)(2,1)S(1)}, u32[]{:S(2)}, u32[]{:S(2)}) async-start(bf16[32,1,168]{2,1,0:T(2,128)(2,1)} %broadcast_in_dim.2), calls=%async_computation.1 | async-start | bytes 65536 | tf_op jit(solution)/shard_map/all_to_all | solution.py:136
  22.2 63.8 %all-to-all-start = ((bf16[32,32,192]{2,1,0:T(8,128)(2,1)}), bf16[32,32,192]{2,1,0:T(8,128)(2,1)S(1)}, u32[]{:S(2)}, u32[]{:S(2)}) async-start(bf16[32,32,192]{2,1,0:T(8,128)(2,1)} %bitcast), calls=%async_computation | async-start | bytes 1048576 | tf_op jit(solution)/shard_map/all_to_all | solution.py:127
  24.8 52.9 %copy-start.7 = (bf16[225792]{0:T(1024)(128)(2,1)S(1)}, bf16[225792]{0:T(1024)(128)(2,1)}, u32[]{:S(2)}) copy-start(bf16[225792]{0:T(1024)(128)(2,1)} %param.19) | copy-start | bytes 1354756
  80.6 4.0 %copy-start.10 = (bf16[32256]{0:T(1024)(128)(2,1)S(1)}, bf16[32256]{0:T(1024)(128)(2,1)}, u32[]{:S(2)}) copy-start(bf16[32256]{0:T(1024)(128)(2,1)} %param.20) | copy-start | bytes 193540
  80.6 4.8 %copy-start.11 = (s32[200,1]{0,1:T(1,128)S(1)}, s32[200,1]{0,1:T(1,128)}, u32[]{:S(2)}) copy-start(s32[200,1]{0,1:T(1,128)} %param.15) | copy-start | bytes 2404
  89.5 1.0 copy-start
  90.5 89.1 %copy-start.4 = (bf16[8,168,168]{2,1,0:T(8,128)(2,1)S(1)}, bf16[8,168,168]{2,1,0:T(8,128)(2,1)}, u32[]{:S(2)}) copy-start(bf16[8,168,168]{2,1,0:T(8,128)(2,1)} %reshape.65) | copy-start | bytes 1354756
  178.8 0.7 copy-start.1
  179.8 3.5 %copy-start.3 = (s32[26,512]{1,0:T(8,128)S(1)}, s32[26,512]{1,0:T(8,128)}, u32[]{:S(2)}) copy-start(s32[26,512]{1,0:T(8,128)} %lists.2) | copy-start | bytes 159748
  183.3 14.1 %copy-start.2 = (f32[168,512]{1,0:T(8,128)S(1)}, f32[168,512]{1,0:T(8,128)}, u32[]{:S(2)}) copy-start(f32[168,512]{1,0:T(8,128)} %copy-done.1) | copy-start | bytes 1032196
  183.3 14.2 %copy-start.5 = (f32[168,512]{1,0:T(8,128)S(1)}, f32[168,512]{1,0:T(8,128)}, u32[]{:S(2)}) copy-start(f32[168,512]{1,0:T(8,128)} %copy.33) | copy-start | bytes 1032196
  183.3 14.2 %copy-start.9 = (bf16[168,192]{1,0:T(8,128)(2,1)S(1)}, bf16[168,192]{1,0:T(8,128)(2,1)}, u32[]{:S(2)}) copy-start(bf16[168,192]{1,0:T(8,128)(2,1)} %reshape.67) | copy-start | bytes 193540

commit v2 on v1

--- a/solution.py
+++ b/solution.py
@@ -1,3 +1,6 @@
+import functools
+import math
+
 import jax
 import jax.numpy as jnp
 from jax import lax
@@ -20,6 +23,46 @@
 
 def dot_t(left, right):
     return lax.dot_general(left, right, (((0,), (0,)), ((), ())), preferred_element_type=F32)
+
+
+def rows_kernel(width, period, lanes, flat, out, wide, placed):
+    groups = wide.shape[0] // lanes
+    wide[...] = flat[...].astype(F32)
+
+    def line(at):
+        return wide[pl.ds(at, groups, stride=lanes), :]
+
+    for row in range(period):
+        start, offset = divmod(row * width, 128)
+        for low in range(0, width, 128):
+            size = min(128, width - low)
+            here = start + low // 128
+            first = line(here)
+            if offset:
+                rest = line(here + 1) if offset + size > 128 else first
+                first = jnp.concatenate([first[:, offset:], rest[:, :offset]], axis=1)
+            placed[low // 128, pl.ds(row, groups, stride=period), :] = first
+    for low in range(0, width, 128):
+        high = min(low + 128, width)
+        out[:, low:high] = placed[low // 128, :, : high - low].astype(BF)
+
+
+def as_rows(flat, width, groups):
+    total = flat.shape[0]
+    period = 128 // math.gcd(width, 128)
+    lanes = width * period // 128
+    return pl.pallas_call(
+        functools.partial(rows_kernel, width, period, lanes),
+        grid=(pl.cdiv(total // (width * period), groups),),
+        in_specs=[pl.BlockSpec((groups * lanes, 128), lambda i: (i, 0))],
+        out_specs=pl.BlockSpec((groups * period, width), lambda i: (i, 0)),
+        out_shape=jax.ShapeDtypeStruct((total // width, width), BF),
+        scratch_shapes=[
+            pltpu.VMEM((groups * lanes, 128), F32),
+            pltpu.VMEM((pl.cdiv(width, 128), groups * period, 128), F32),
+        ],
+        compiler_params=pltpu.CompilerParams(vmem_limit_bytes=48 * 2**20),
+    )(flat.reshape(total // 128, 128))
 
 
 def far_kernel(lists, m2l, pool, top, far, top_far, picked):
@@ -114,27 +157,28 @@
     near_count = near_lists.shape[0]
     ewidth = point_to_mult.shape[0] // dwidth
     p2m = point_to_mult.reshape(dwidth, ewidth)
-    m2m = mult_to_mult.reshape(8, ewidth, ewidth)
-    m2l_rows = mult_to_local.reshape(offset_count * ewidth, ewidth)
-    l2l = local_to_local.reshape(8, ewidth, ewidth)
+    m2m = as_rows(mult_to_mult, ewidth, 48).reshape(8, ewidth, ewidth)
+    m2l_rows = as_rows(mult_to_local, ewidth, 240)
+    l2l = as_rows(local_to_local, ewidth, 48).reshape(8, ewidth, ewidth)
     l2p = local_to_point.reshape(ewidth, dwidth)
-    p2p_rows = point_to_point.reshape((near_count + 1) * dwidth, dwidth)
+    p2p_rows = as_rows(point_to_point, dwidth, 864)
 
     sends = ghost_sends[:, None] == lax.broadcasted_iota(jnp.int32, (1, leaf_count), 1)
     packed = lax.dot_general(
         sends.astype(BF), densities, (((1,), (1,)), ((), ())), preferred_element_type=F32
     ).astype(BF)
-    arrived = lax.all_to_all(packed, axes, split_axis=0, concat_axis=0, tiled=True)
-
     mult_rows = jnp.einsum("dl,de->le", densities, p2m, preferred_element_type=F32).astype(BF)
     level_mult = mult_rows.T
     for level_index in range(LEVELS):
         grouped = level_mult.reshape(ewidth, -1, 8)
         level_mult = jnp.einsum("ebk,kef->fb", grouped, m2m, preferred_element_type=F32).astype(BF)
-    mine = level_mult.T
-    copies = jnp.broadcast_to(mine[None], (devices,) + mine.shape)
-    top_boxes = lax.all_to_all(copies, axes, split_axis=0, concat_axis=0, tiled=True)
-    top_boxes = top_boxes.reshape(-1, ewidth)
+    ghosts = ghost_sends.shape[0] // devices
+    tops = jnp.pad(level_mult.T, ((0, 0), (0, dwidth - ewidth)))
+    tops = jnp.broadcast_to(tops[None], (devices,) + tops.shape)
+    leaving = jnp.concatenate([packed.reshape(devices, ghosts, dwidth), tops], axis=1)
+    landed = lax.all_to_all(leaving, axes, split_axis=0, concat_axis=0, tiled=True)
+    arrived = landed[:, :ghosts].reshape(devices * ghosts, dwidth)
+    top_boxes = landed[:, ghosts:, :ewidth].reshape(-1, ewidth)
     top_hot = top_lists == lax.broadcasted_iota(jnp.int32, (1, top_boxes.shape[0]), 1)
     top_picked = jnp.dot(top_hot.astype(BF), top_boxes, preferred_element_type=F32).astype(BF)
 

time: 199 us -> 169 us (0.85)
  local copies, waits for them, and re-layouts: 73.3 us -> 16.7 us
  Pallas kernels: 102 us -> 136 us
  waiting for transfers between devices: 5.52 us -> 0.01 us
  starting transfers between devices: 9.9 us -> 7.41 us
    reshape x4 -> x1, local copies, waits for them, and re-layouts: 62.8 us -> 1.98 us  [shards(): arrived = landed[:, :ghosts].reshape(devices * ghosts, dwidth)]
    pallas_call x0 -> x4, Pallas kernels: none -> 33.8 us  [as_rows(): pl.pallas_call(functools.partial(rows_kernel, width, period, lanes), grid...]
    all_to_all x2 -> x1, waiting for transfers between devices: 5.52 us -> 0.01 us  [shards(): lax.all_to_all(leaving, axes, split_axis=0, concat_axis=0, tiled=True)]
    slice x0 -> x2, local copies, waits for them, and re-layouts: none -> 2.83 us  [the longest x1 1.91 us: shards(): arrived = landed[:, :ghosts].reshape(devices * ghosts, dwidth)]
    all_to_all x2 -> x1, starting transfers between devices: 9.9 us -> 7.41 us  [shards(): lax.all_to_all(leaving, axes, split_axis=0, concat_axis=0, tiled=True)]
  transfers between devices with their start and end apart: 2 -> 1, of which waited for: 1 -> 0; matrix products, arithmetic and copies ran while one was open for 32% -> 1% of each run, Pallas kernels for 0% -> 19%
where the time goes in v2:
time: 169 us; the launch traced here: 168 us
  Pallas kernels  136 us (80%)
  local copies, waits for them, and re-layouts  16.7 us (10%)
  starting transfers between devices  7.41 us (4%)
  matrix products  5.8 us (3%)
  other arithmetic  1.87 us (1%)
    pallas_call x1, Pallas kernels, far_call(): pl.pallas_call(far_kernel, grid=(offsets // BLOCK,), in_specs=[pl.BlockSp...  88.2 us
    pallas_call x4, Pallas kernels, as_rows(): pl.pallas_call(functools.partial(rows_kernel, width, period, lanes), grid...  33.8 us
    pallas_call x1, Pallas kernels, near_call(): pl.pallas_call(near_kernel, out_shape=jax.ShapeDtypeStruct((dwidth, leave...  14.1 us
    all_to_all x1, starting transfers between devices, shards(): lax.all_to_all(leaving, axes, split_axis=0, concat_axis=0, tiled=True)  7.41 us
    unnamed x32, local copies, waits for them, and re-layouts  3.77 us
  transfers between devices with their start and end apart: 1, of which 0 were waited for; matrix products, arithmetic and copies ran while one was open for 1% of the time, Pallas kernels for 19%

profile of v2, /device:TPU:0, one launch (start us, length us, event | category | flops | bytes accessed | tf_op | source)
XLA Modules:
  0.0 168.2 jit_solution(6238236686980519049)
XLA Ops:
  0.0 1.0 copy-done.3
  1.0 1.3 shard_map.110
  2.3 1.1 reshape.69
  3.5 0.6 copy-done.12
  4.1 0.2 convolution_convert_fusion.1
  4.5 0.3 fusion.6
  4.8 0.2 fusion.8
  5.0 0.3 fusion.17
  5.4 0.7 fusion.2
  6.3 1.0 pad_maximum_fusion
  7.3 7.4 %all-to-all-start = ((bf16[32,33,192]{2,1,0:T(8,128)(2,1)}), bf16[32,33,192]{2,1,0:T(8,128)(2,1)}, u32[]{:S(2)}, u32[]{:S(2)}) async-start(bf16[32,33,192]{2,1,0:T(8,128)(2,1)} %pad_maximum_fusion), calls=%async_computation | async-start | bytes 1310720 | tf_op jit(solution)/shard_map/all_to_all | solution.py:179
  14.7 29.7 %shard_map.112.m2l = bf16[33600,168]{1,0:T(8,128)(2,1)} custom-call(bf16[44100,128]{1,0:T(8,128)(2,1)} %bitcast.90), custom_call_target="tpu_custom_call" | custom-call | tf_op jit(solution)/shard_map/pallas_call | solution.py:54
  44.4 1.3 shard_map.114
  45.7 1.5 shard_map.109.p2p
  47.3 1.6 reshape.81
  48.9 1.9 %slice.8 = bf16[32,32,192]{2,1,0:T(8,128)(2,1)} slice(bf16[32,33,192]{2,1,0:T(8,128)(2,1)} %all-to-all-done), slice={[0:32], [0:32], [0:192]} | slice | bytes 786432 | tf_op jit(solution)/shard_map/slice | solution.py:180
  50.8 2.0 %copy.18 = bf16[1024,192]{0,1:T(8,128)(2,1)} copy(bf16[1024,192]{1,0:T(8,128)(2,1)} %bitcast.92) | data formatting | bytes 786432 | tf_op jit(solution)/shard_map/reshape | solution.py:180
  52.8 2.2 %fusion.pool = bf16[168,1536]{1,0:T(8,128)(2,1)} fusion(bf16[192,168]{1,0:T(8,128)(2,1)} %copy-done.12, bf16[192,1024]{1,0:T(8,128)(2,1)} %bitcast.94, bf16[192,512]{1,0:T(8,128)(2,1)S(1)} %copy-done.11), kind=kOutput, calls=%fused_computation.1 | convolution fusion | flops 100528128 | bytes 1170432 | tf_op jit(solution)/shard_map/dl,de->el/dot_general | solution.py:186
  55.0 0.9 pad_maximum_fusion.1.pool
  55.8 0.9 slice.9
  56.8 0.3 convolution_convert_fusion.2
  57.1 0.8 copy.19
  57.8 1.2 reshape.90.top
  59.0 1.0 copy-done.2
  60.0 1.0 copy-done.5
  61.0 88.2 %shard_map.113 = (f32[168,512]{1,0:T(8,128)S(1)}, f32[1,168]{1,0:T(1,128)S(1)}) custom-call(s32[200,512]{1,0:T(8,128)S(1)} %copy-done.5, bf16[33600,168]{1,0:T(8,128)(2,1)} %shard_map.112.m2l, bf16[168,1536]{1,0:T(8,128)(2,1)S(1)} %copy-done.2, bf16[25,1,1344]{2,1,0:T(2,128)(2,1)S(1)} %reshape.90.top), custom_call_target="tpu_custom_call" | custom-call | tf_op jit(solution)/shard_map/pallas_call | solution.py:93
  149.4 0.2 fusion.5
  149.6 0.3 convolution_bitcast_fusion
  149.9 1.1 copy.47
  151.0 1.9 %copy.23 = f32[168,512]{1,0:T(8,128)} copy(f32[168,512]{0,1:T(8,128)} %bitcast.93) | data formatting | bytes 688128 | tf_op jit(solution)/shard_map/reshape | solution.py:200
  153.0 14.1 %shard_map.111 = f32[192,512]{1,0:T(8,128)S(1)} custom-call(s32[26,512]{1,0:T(8,128)S(1)} %copy-done.8, bf16[5184,192]{1,0:T(8,128)(2,1)S(1)} %shard_map.109.p2p, bf16[192,1536]{1,0:T(8,128)(2,1)S(1)} %copy-done), custom_call_target="tpu_custom_call" | custom-call | tf_op jit(solution)/shard_map/pallas_call | solution.py:132
  167.2 1.0 fusion.3
  (36 shorter events, 0.7 us)
Async XLA Ops:
  0.0 1.0 copy-start.3
  1.0 3.1 %copy-start.11 = (bf16[192,512]{1,0:T(8,128)(2,1)S(1)}, bf16[192,512]{1,0:T(8,128)(2,1)}, u32[]{:S(2)}) copy-start(bf16[192,512]{1,0:T(8,128)(2,1)} %param.11) | copy-start | bytes 589828
  3.5 0.6 copy-start.12
  4.5 0.9 copy-start.15
  7.3 41.6 %all-to-all-start = ((bf16[32,33,192]{2,1,0:T(8,128)(2,1)}), bf16[32,33,192]{2,1,0:T(8,128)(2,1)}, u32[]{:S(2)}, u32[]{:S(2)}) async-start(bf16[32,33,192]{2,1,0:T(8,128)(2,1)} %pad_maximum_fusion), calls=%async_computation | async-start | bytes 1310720 | tf_op jit(solution)/shard_map/all_to_all | solution.py:179
  14.7 29.7 %copy-start.4 = (bf16[225792]{0:T(1024)(128)(2,1)S(1)}, bf16[225792]{0:T(1024)(128)(2,1)}, u32[]{:S(2)}) copy-start(bf16[225792]{0:T(1024)(128)(2,1)} %param.19) | copy-start | bytes 1354756
  14.7 31.0 %copy-start.1 = (bf16[995328]{0:T(1024)(128)(2,1)S(1)}, bf16[995328]{0:T(1024)(128)(2,1)}, u32[]{:S(2)}) copy-start(bf16[995328]{0:T(1024)(128)(2,1)} %param.21) | copy-start | bytes 5971972
  52.8 2.2 %copy-start.9 = (bf16[1024,192]{0,1:T(8,128)(2,1)S(1)}, bf16[1024,192]{0,1:T(8,128)(2,1)}, u32[]{:S(2)}) copy-start(bf16[1024,192]{0,1:T(8,128)(2,1)} %copy.18) | copy-start | bytes 1179652
  52.8 4.0 %copy-start.14 = (s32[200,1]{0,1:T(1,128)S(1)}, s32[200,1]{0,1:T(1,128)}, u32[]{:S(2)}) copy-start(s32[200,1]{0,1:T(1,128)} %param.15) | copy-start | bytes 2404
  59.0 1.0 copy-start.2
  60.0 1.0 copy-start.5
  149.2 0.7 copy-start.6
  149.6 3.3 %copy-start.8 = (s32[26,512]{1,0:T(8,128)S(1)}, s32[26,512]{1,0:T(8,128)}, u32[]{:S(2)}) copy-start(s32[26,512]{1,0:T(8,128)} %lists.2) | copy-start | bytes 159748
  149.9 3.0 %copy-start = (bf16[192,1536]{1,0:T(8,128)(2,1)S(1)}, bf16[192,1536]{1,0:T(8,128)(2,1)}, u32[]{:S(2)}) copy-start(bf16[192,1536]{1,0:T(8,128)(2,1)} %pad_maximum_fusion.1.pool) | copy-start | bytes 1769476
  153.0 14.2 %copy-start.7 = (f32[168,512]{1,0:T(8,128)S(1)}, f32[168,512]{1,0:T(8,128)}, u32[]{:S(2)}) copy-start(f32[168,512]{1,0:T(8,128)} %copy-done.6) | copy-start | bytes 1032196
  153.0 14.2 %copy-start.10 = (f32[168,512]{1,0:T(8,128)S(1)}, f32[168,512]{1,0:T(8,128)}, u32[]{:S(2)}) copy-start(f32[168,512]{1,0:T(8,128)} %copy.23) | copy-start | bytes 1032196
  153.0 14.2 %copy-start.13 = (bf16[168,192]{1,0:T(8,128)(2,1)S(1)}, bf16[168,192]{1,0:T(8,128)(2,1)}, u32[]{:S(2)}) copy-start(bf16[168,192]{1,0:T(8,128)(2,1)} %reshape.81) | copy-start | bytes 193540

commit v3 on v2

--- a/solution.py
+++ b/solution.py
@@ -12,13 +12,29 @@
 BLOCK = 8
 BF = jnp.bfloat16
 F32 = jnp.float32
+F8 = jnp.float8_e4m3fn
 
 
 def one_hot(row, depth):
     shape = (depth, row.shape[1])
     key = jnp.broadcast_to(row.astype(jnp.int16), shape)
     ids = lax.broadcasted_iota(jnp.int16, shape, 0)
-    return jnp.where(key == ids, jnp.ones(shape, BF), jnp.zeros(shape, BF))
+    return jnp.where(key == ids, jnp.ones(shape, BF), jnp.zeros(shape, BF)).astype(F8)
+
+
+def pick(pool, back, row):
+    both = jnp.dot(pool[...], one_hot(row, pool.shape[1]), preferred_element_type=F32)
+    width = both.shape[0] // 2
+    return (both[:width] + both[width:]) * back[...]
+
+
+def split(pool):
+    values = pool.astype(F32)
+    largest = jnp.maximum(jnp.max(jnp.abs(values), axis=1, keepdims=True), 1e-30)
+    unit = jnp.exp2(jnp.floor(jnp.log2(largest)) - 6.0)
+    scaled = values / unit
+    high = lax.reduce_precision(scaled, 8, 3)
+    return jnp.concatenate([high, scaled - high], axis=0).astype(F8), unit
 
 
 def dot_t(left, right):
@@ -27,6 +43,7 @@
 
 def rows_kernel(width, period, lanes, flat, out, wide, placed):
     groups = wide.shape[0] // lanes
+    odd = placed.shape[1] // groups
     wide[...] = flat[...].astype(F32)
 
     def line(at):
@@ -41,16 +58,22 @@
             if offset:
                 rest = line(here + 1) if offset + size > 128 else first
                 first = jnp.concatenate([first[:, offset:], rest[:, :offset]], axis=1)
-            placed[low // 128, pl.ds(row, groups, stride=period), :] = first
+            placed[low // 128, pl.ds(row, groups, stride=odd), :] = first
     for low in range(0, width, 128):
         high = min(low + 128, width)
-        out[:, low:high] = placed[low // 128, :, : high - low].astype(BF)
+        if odd == period:
+            out[:, low:high] = placed[low // 128, :, : high - low].astype(BF)
+            continue
+        for group in range(groups):
+            run = placed[low // 128, pl.ds(group * odd, period), : high - low]
+            out[group * period : (group + 1) * period, low:high] = run.astype(BF)
 
 
 def as_rows(flat, width, groups):
     total = flat.shape[0]
     period = 128 // math.gcd(width, 128)
     lanes = width * period // 128
+    odd = period + (period % 16 == 0)
     return pl.pallas_call(
         functools.partial(rows_kernel, width, period, lanes),
         grid=(pl.cdiv(total // (width * period), groups),),
@@ -59,14 +82,14 @@
         out_shape=jax.ShapeDtypeStruct((total // width, width), BF),
         scratch_shapes=[
             pltpu.VMEM((groups * lanes, 128), F32),
-            pltpu.VMEM((pl.cdiv(width, 128), groups * period, 128), F32),
+            pltpu.VMEM((pl.cdiv(width, 128), groups * odd, 128), F32),
         ],
         compiler_params=pltpu.CompilerParams(vmem_limit_bytes=48 * 2**20),
     )(flat.reshape(total // 128, 128))
 
 
-def far_kernel(lists, m2l, pool, top, far, top_far, picked):
-    ewidth, depth = pool.shape
+def far_kernel(lists, m2l, pool, back, top, far, top_far, picked):
+    ewidth = back.shape[0]
 
     @pl.when(pl.program_id(0) == 0)
     def _():
@@ -77,8 +100,7 @@
     def _(pair):
         both = []
         for half in range(2):
-            hot = one_hot(lists[pl.ds(2 * pair + half, 1), :], depth)
-            both.append(jnp.dot(pool[...], hot, preferred_element_type=F32))
+            both.append(pick(pool, back, lists[pl.ds(2 * pair + half, 1), :]))
         start = pl.multiple_of(pair * (2 * ewidth), 16)
         picked[pl.ds(start, 2 * ewidth), :] = jnp.concatenate(both, axis=0).astype(BF)
 
@@ -86,9 +108,9 @@
     top_far[...] += jnp.dot(top[0], m2l[...], preferred_element_type=F32)
 
 
-def far_call(far_lists, m2l_rows, pool, top):
+def far_call(far_lists, m2l_rows, pool, back, top):
     offsets, leaves = far_lists.shape
-    ewidth, depth = pool.shape
+    ewidth = back.shape[0]
     rows = BLOCK * ewidth
     return pl.pallas_call(
         far_kernel,
@@ -96,7 +118,8 @@
         in_specs=[
             pl.BlockSpec((BLOCK, leaves), lambda i: (i, 0)),
             pl.BlockSpec((rows, ewidth), lambda i: (i, 0)),
-            pl.BlockSpec((ewidth, depth), lambda i: (0, 0)),
+            pl.BlockSpec(pool.shape, lambda i: (0, 0)),
+            pl.BlockSpec(back.shape, lambda i: (0, 0)),
             pl.BlockSpec((1, 1, rows), lambda i: (i, 0, 0)),
         ],
         out_specs=[
@@ -109,32 +132,31 @@
         ],
         scratch_shapes=[pltpu.VMEM((rows, leaves), BF)],
         compiler_params=pltpu.CompilerParams(vmem_limit_bytes=48 * 2**20),
-    )(far_lists, m2l_rows, pool, top)
-
-
-def near_kernel(lists, p2p, pool, out, picked):
-    dwidth, depth = pool.shape
+    )(far_lists, m2l_rows, pool, back, top)
+
+
+def near_kernel(lists, p2p, pool, back, own, out, picked):
+    dwidth = back.shape[0]
     classes, leaves = lists.shape
 
     @pl.loop(0, classes)
     def _(c):
-        hot = one_hot(lists[pl.ds(c, 1), :], depth)
-        found = jnp.dot(pool[...], hot, preferred_element_type=F32).astype(BF)
+        found = pick(pool, back, lists[pl.ds(c, 1), :]).astype(BF)
         picked[pl.ds(pl.multiple_of(c * dwidth, 16), dwidth), :] = found
 
-    picked[classes * dwidth :, :] = pool[:, :leaves]
+    picked[classes * dwidth :, :] = own[...]
     out[...] = dot_t(p2p[...], picked[...])
 
 
-def near_call(near_lists, p2p_rows, pool):
+def near_call(near_lists, p2p_rows, pool, back, own):
     classes, leaves = near_lists.shape
-    dwidth, depth = pool.shape
+    dwidth = own.shape[0]
     return pl.pallas_call(
         near_kernel,
         out_shape=jax.ShapeDtypeStruct((dwidth, leaves), F32),
         scratch_shapes=[pltpu.VMEM(((classes + 1) * dwidth, leaves), BF)],
         compiler_params=pltpu.CompilerParams(vmem_limit_bytes=48 * 2**20),
-    )(near_lists, p2p_rows, pool)
+    )(near_lists, p2p_rows, pool, back, own)
 
 
 def shards(
@@ -187,10 +209,10 @@
     far, top_far = far_call(
         far_lists,
         m2l_rows,
-        mult_pool,
+        *split(mult_pool),
         top_picked.reshape(offset_count // BLOCK, 1, BLOCK * ewidth),
     )
-    near = near_call(near_lists, p2p_rows, dens_pool)
+    near = near_call(near_lists, p2p_rows, *split(dens_pool), densities)
 
     local_exp = top_far.T.astype(BF)
     leaf_far = None

time: 169 us -> 163 us (0.964)
  Pallas kernels: 136 us -> 123 us
  other arithmetic: 1.87 us -> 7.03 us
    pallas_call x4, Pallas kernels: 33.8 us -> 23.7 us  [as_rows(): pl.pallas_call(functools.partial(rows_kernel, width, period, lanes), grid...]
    another operation x0 -> x2, other arithmetic: none -> 2.9 us
    concatenate x1 -> x2, other arithmetic: 0.87 us -> 2.9 us  [split(): return (jnp.concatenate([high, scaled - high], axis=0).astype(F8), unit)]
    unnamed x32 -> x36, local copies, waits for them, and re-layouts: 3.77 us -> 3.57 us
  transfers between devices with their start and end apart: 1 -> 1, of which waited for: 0 -> 0; matrix products, arithmetic and copies ran while one was open for 1% -> 1% of each run, Pallas kernels for 19% -> 14%
where the time goes in v3:
time: 163 us; the launch traced here: 162 us
  Pallas kernels  123 us (75%)
  local copies, waits for them, and re-layouts  18 us (11%)
  starting transfers between devices  7.42 us (5%)
  other arithmetic  7.03 us (4%)
  matrix products  5.77 us (4%)
    pallas_call x1, Pallas kernels, far_call(): pl.pallas_call(far_kernel, grid=(offsets // BLOCK,), in_specs=[pl.BlockSp...  86.9 us
    pallas_call x4, Pallas kernels, as_rows(): pl.pallas_call(functools.partial(rows_kernel, width, period, lanes), grid...  23.7 us
    pallas_call x1, Pallas kernels, near_call(): pl.pallas_call(near_kernel, out_shape=jax.ShapeDtypeStruct((dwidth, leave...  12.8 us
    all_to_all x1, starting transfers between devices, shards(): lax.all_to_all(leaving, axes, split_axis=0, concat_axis=0, tiled=True)  7.42 us
    unnamed x36, local copies, waits for them, and re-layouts  3.57 us
  transfers between devices with their start and end apart: 1, of which 0 were waited for; matrix products, arithmetic and copies ran while one was open for 1% of the time, Pallas kernels for 14%

profile of v3, /device:TPU:0, one launch (start us, length us, event | category | flops | bytes accessed | tf_op | source)
XLA Modules:
  0.0 162.0 jit_solution(743301277157558829)
XLA Ops:
  0.0 1.1 copy-done.3
  1.1 0.9 shard_map.110
  2.0 0.3 reshape.145
  2.3 0.6 copy-done.13
  3.3 0.3 fusion.8
  3.8 0.3 fusion.20
  4.1 0.7 fusion.2
  5.1 1.0 pad_maximum_fusion
  6.1 7.4 %all-to-all-start = ((bf16[32,33,192]{2,1,0:T(8,128)(2,1)}), bf16[32,33,192]{2,1,0:T(8,128)(2,1)}, u32[]{:S(2)}, u32[]{:S(2)}) async-start(bf16[32,33,192]{2,1,0:T(8,128)(2,1)} %pad_maximum_fusion), calls=%async_computation | async-start | bytes 1310720 | tf_op jit(solution)/shard_map/all_to_all | solution.py:201
  13.5 20.4 %shard_map.112.m2l = bf16[33600,168]{1,0:T(8,128)(2,1)} custom-call(bf16[44100,128]{1,0:T(8,128)(2,1)} %bitcast.93), custom_call_target="tpu_custom_call" | custom-call | tf_op jit(solution)/shard_map/pallas_call | solution.py:77
  33.9 0.9 shard_map.114
  34.8 1.5 shard_map.109.p2p
  36.4 1.6 reshape.157
  38.0 1.9 %slice.8 = bf16[32,32,192]{2,1,0:T(8,128)(2,1)} slice(bf16[32,33,192]{2,1,0:T(8,128)(2,1)} %all-to-all-done), slice={[0:32], [0:32], [0:192]} | slice | bytes 786432 | tf_op jit(solution)/shard_map/slice | solution.py:202
  39.9 2.0 %copy.18 = bf16[1024,192]{0,1:T(8,128)(2,1)} copy(bf16[1024,192]{1,0:T(8,128)(2,1)} %bitcast.98) | data formatting | bytes 786432 | tf_op jit(solution)/shard_map/reshape | solution.py:202
  41.9 1.5 abs_reduce_fusion
  43.6 1.4 reduce-precision_convert_fusion.1
  45.0 0.7 copy.21.back
  45.8 0.9 slice.9
  46.7 0.9 convolution_convert_fusion.2
  47.6 1.6 %copy.20 = bf16[200,168]{1,0:T(8,128)(2,1)} copy(bf16[200,168]{0,1:T(8,128)(2,1)} %convolution_convert_fusion.2) | data formatting | bytes 134400 | tf_op jit(solution)/shard_map/convert_element_type | solution.py:205
  49.2 1.8 %reshape.176.top = bf16[25,1,1344]{2,1,0:T(2,128)(2,1)} reshape(bf16[200,168]{1,0:T(8,128)(2,1)} %copy.20) | data formatting | bytes 134400 | tf_op jit(solution)/shard_map/reshape | solution.py:213
  51.1 1.5 pad_maximum_fusion.3.pool
  52.5 0.9 copy-done.2
  53.5 0.9 copy-done.6
  54.3 86.9 %shard_map.113 = (f32[168,512]{1,0:T(8,128)S(1)}, f32[1,168]{1,0:T(1,128)S(1)}) custom-call(s32[200,512]{1,0:T(8,128)S(1)} %copy-done.5, bf16[33600,168]{1,0:T(8,128)(2,1)} %shard_map.112.m2l, f8e4m3fn[336,1536]{1,0:T(8,128)(4,1)S(1)} %pad_maximum_fusion.3.pool, f32[168,1]{1,0:T(8,128)S(1)} %copy-done.6, bf16[25,1,1344]{2,1,0:T(2,128)(2,1)S(1)} %copy-done.2), custom_call_target="tpu_custom_call" | custom-call | tf_op jit(solution)/shard_map/pallas_call | solution.py:115
  142.0 1.1 copy.49
  143.1 2.0 %copy.25 = f32[168,512]{1,0:T(8,128)} copy(f32[168,512]{0,1:T(8,128)} %bitcast.99) | data formatting | bytes 688128 | tf_op jit(solution)/shard_map/reshape | solution.py:222
  145.1 1.5 reduce-precision_convert_fusion
  146.7 1.4 pad_maximum_fusion.2.pool
  148.2 12.8 %shard_map.111 = f32[192,512]{1,0:T(8,128)S(1)} custom-call(s32[26,512]{1,0:T(8,128)S(1)} %copy-done.9, bf16[5184,192]{1,0:T(8,128)(2,1)S(1)} %shard_map.109.p2p, f8e4m3fn[384,1536]{1,0:T(32,128)(4,1)S(1)} %pad_maximum_fusion.2.pool, f32[192,1]{1,0:T(8,128)S(1)} %copy.19.back, bf16[192,512]{1,0:T(8,128)(2,1)S(1)} %copy-done), custom_call_target="tpu_custom_call" | custom-call | tf_op jit(solution)/shard_map/pallas_call | solution.py:154
  161.0 1.0 fusion.3
  (48 shorter events, 2.0 us)
Async XLA Ops:
  0.0 2.9 %copy-start = (bf16[192,512]{1,0:T(8,128)(2,1)S(1)}, bf16[192,512]{1,0:T(8,128)(2,1)}, u32[]{:S(2)}) copy-start(bf16[192,512]{1,0:T(8,128)(2,1)} %own.1) | copy-start | bytes 589828
  0.0 1.1 copy-start.3
  1.1 0.9 copy-start.15
  2.3 0.6 copy-start.13
  3.3 0.9 copy-start.17
  6.1 31.9 %all-to-all-start = ((bf16[32,33,192]{2,1,0:T(8,128)(2,1)}), bf16[32,33,192]{2,1,0:T(8,128)(2,1)}, u32[]{:S(2)}, u32[]{:S(2)}) async-start(bf16[32,33,192]{2,1,0:T(8,128)(2,1)} %pad_maximum_fusion), calls=%async_computation | async-start | bytes 1310720 | tf_op jit(solution)/shard_map/all_to_all | solution.py:201
  13.5 20.4 %copy-start.4 = (bf16[225792]{0:T(1024)(128)(2,1)S(1)}, bf16[225792]{0:T(1024)(128)(2,1)}, u32[]{:S(2)}) copy-start(bf16[225792]{0:T(1024)(128)(2,1)} %param.19) | copy-start | bytes 1354756
  13.5 21.3 %copy-start.1 = (bf16[995328]{0:T(1024)(128)(2,1)S(1)}, bf16[995328]{0:T(1024)(128)(2,1)}, u32[]{:S(2)}) copy-start(bf16[995328]{0:T(1024)(128)(2,1)} %param.21) | copy-start | bytes 5971972
  41.9 1.5 copy-start.10
  43.4 3.3 %copy-start.16 = (s32[200,1]{0,1:T(1,128)S(1)}, s32[200,1]{0,1:T(1,128)}, u32[]{:S(2)}) copy-start(s32[200,1]{0,1:T(1,128)} %param.15) | copy-start | bytes 2404
  51.1 1.5 copy-start.5
  52.5 0.9 copy-start.2
  53.4 0.9 copy-start.6
  141.3 0.7 copy-start.7
  142.0 3.1 %copy-start.11 = (bf16[1024,192]{0,1:T(8,128)(2,1)S(1)}, bf16[1024,192]{0,1:T(8,128)(2,1)}, u32[]{:S(2)}) copy-start(bf16[1024,192]{0,1:T(8,128)(2,1)} %copy.18) | copy-start | bytes 1179652
  145.1 3.1 %copy-start.9 = (s32[26,512]{1,0:T(8,128)S(1)}, s32[26,512]{1,0:T(8,128)}, u32[]{:S(2)}) copy-start(s32[26,512]{1,0:T(8,128)} %lists.2) | copy-start | bytes 159748
  148.2 12.8 %copy-start.8 = (f32[168,512]{1,0:T(8,128)S(1)}, f32[168,512]{1,0:T(8,128)}, u32[]{:S(2)}) copy-start(f32[168,512]{1,0:T(8,128)} %copy-done.7) | copy-start | bytes 1032196
  148.2 12.8 %copy-start.12 = (f32[168,512]{1,0:T(8,128)S(1)}, f32[168,512]{1,0:T(8,128)}, u32[]{:S(2)}) copy-start(f32[168,512]{1,0:T(8,128)} %copy.25) | copy-start | bytes 1032196
  148.2 12.8 %copy-start.14 = (bf16[168,192]{1,0:T(8,128)(2,1)S(1)}, bf16[168,192]{1,0:T(8,128)(2,1)}, u32[]{:S(2)}) copy-start(bf16[168,192]{1,0:T(8,128)(2,1)} %reshape.157) | copy-start | bytes 193540

commit v4 on v3

--- a/solution.py
+++ b/solution.py
@@ -12,29 +12,24 @@
 BLOCK = 8
 BF = jnp.bfloat16
 F32 = jnp.float32
-F8 = jnp.float8_e4m3fn
 
 
 def one_hot(row, depth):
-    shape = (depth, row.shape[1])
-    key = jnp.broadcast_to(row.astype(jnp.int16), shape)
+    leaves = row.shape[1]
+    shape = (128, leaves)
+    key = jnp.broadcast_to((row & 127).astype(jnp.int16), shape)
     ids = lax.broadcasted_iota(jnp.int16, shape, 0)
-    return jnp.where(key == ids, jnp.ones(shape, BF), jnp.zeros(shape, BF)).astype(F8)
-
-
-def pick(pool, back, row):
-    both = jnp.dot(pool[...], one_hot(row, pool.shape[1]), preferred_element_type=F32)
-    width = both.shape[0] // 2
-    return (both[:width] + both[width:]) * back[...]
-
-
-def split(pool):
-    values = pool.astype(F32)
-    largest = jnp.maximum(jnp.max(jnp.abs(values), axis=1, keepdims=True), 1e-30)
-    unit = jnp.exp2(jnp.floor(jnp.log2(largest)) - 6.0)
-    scaled = values / unit
-    high = lax.reduce_precision(scaled, 8, 3)
-    return jnp.concatenate([high, scaled - high], axis=0).astype(F8), unit
+    low = jnp.where(key == ids, jnp.ones(shape, BF), jnp.zeros(shape, BF))
+    high = jnp.broadcast_to(row >> 7, (16, leaves))
+    parts = []
+    for tile in range(depth // 128):
+        here = jnp.where(high == tile, 1.0, 0.0).astype(BF)
+        parts += [low[at : at + 16] * here for at in range(0, 128, 16)]
+    return jnp.concatenate(parts, axis=0)
+
+
+def pick(pool, row):
+    return jnp.dot(pool[...], one_hot(row, pool.shape[1]), preferred_element_type=F32)
 
 
 def dot_t(left, right):
@@ -88,8 +83,8 @@
     )(flat.reshape(total // 128, 128))
 
 
-def far_kernel(lists, m2l, pool, back, top, far, top_far, picked):
-    ewidth = back.shape[0]
+def far_kernel(lists, m2l, pool, top, far, top_far, picked):
+    ewidth = pool.shape[0]
 
     @pl.when(pl.program_id(0) == 0)
     def _():
@@ -100,7 +95,7 @@
     def _(pair):
         both = []
         for half in range(2):
-            both.append(pick(pool, back, lists[pl.ds(2 * pair + half, 1), :]))
+            both.append(pick(pool, lists[pl.ds(2 * pair + half, 1), :]))
         start = pl.multiple_of(pair * (2 * ewidth), 16)
         picked[pl.ds(start, 2 * ewidth), :] = jnp.concatenate(both, axis=0).astype(BF)
 
@@ -108,9 +103,9 @@
     top_far[...] += jnp.dot(top[0], m2l[...], preferred_element_type=F32)
 
 
-def far_call(far_lists, m2l_rows, pool, back, top):
+def far_call(far_lists, m2l_rows, pool, top):
     offsets, leaves = far_lists.shape
-    ewidth = back.shape[0]
+    ewidth = pool.shape[0]
     rows = BLOCK * ewidth
     return pl.pallas_call(
         far_kernel,
@@ -119,7 +114,6 @@
             pl.BlockSpec((BLOCK, leaves), lambda i: (i, 0)),
             pl.BlockSpec((rows, ewidth), lambda i: (i, 0)),
             pl.BlockSpec(pool.shape, lambda i: (0, 0)),
-            pl.BlockSpec(back.shape, lambda i: (0, 0)),
             pl.BlockSpec((1, 1, rows), lambda i: (i, 0, 0)),
         ],
         out_specs=[
@@ -132,23 +126,23 @@
         ],
         scratch_shapes=[pltpu.VMEM((rows, leaves), BF)],
         compiler_params=pltpu.CompilerParams(vmem_limit_bytes=48 * 2**20),
-    )(far_lists, m2l_rows, pool, back, top)
-
-
-def near_kernel(lists, p2p, pool, back, own, out, picked):
-    dwidth = back.shape[0]
+    )(far_lists, m2l_rows, pool, top)
+
+
+def near_kernel(lists, p2p, pool, own, out, picked):
+    dwidth = pool.shape[0]
     classes, leaves = lists.shape
 
     @pl.loop(0, classes)
     def _(c):
-        found = pick(pool, back, lists[pl.ds(c, 1), :]).astype(BF)
+        found = pick(pool, lists[pl.ds(c, 1), :]).astype(BF)
         picked[pl.ds(pl.multiple_of(c * dwidth, 16), dwidth), :] = found
 
     picked[classes * dwidth :, :] = own[...]
     out[...] = dot_t(p2p[...], picked[...])
 
 
-def near_call(near_lists, p2p_rows, pool, back, own):
+def near_call(near_lists, p2p_rows, pool, own):
     classes, leaves = near_lists.shape
     dwidth = own.shape[0]
     return pl.pallas_call(
@@ -156,7 +150,7 @@
         out_shape=jax.ShapeDtypeStruct((dwidth, leaves), F32),
         scratch_shapes=[pltpu.VMEM(((classes + 1) * dwidth, leaves), BF)],
         compiler_params=pltpu.CompilerParams(vmem_limit_bytes=48 * 2**20),
-    )(near_lists, p2p_rows, pool, back, own)
+    )(near_lists, p2p_rows, pool, own)
 
 
 def shards(
@@ -195,24 +189,31 @@
         grouped = level_mult.reshape(ewidth, -1, 8)
         level_mult = jnp.einsum("ebk,kef->fb", grouped, m2m, preferred_element_type=F32).astype(BF)
     ghosts = ghost_sends.shape[0] // devices
-    tops = jnp.pad(level_mult.T, ((0, 0), (0, dwidth - ewidth)))
+    own_tops = level_mult.shape[1]
+    span = ghosts + 8 * pl.cdiv(own_tops, 8)
+    tops = jnp.pad(level_mult.T, ((0, span - ghosts - own_tops), (0, dwidth - ewidth)))
     tops = jnp.broadcast_to(tops[None], (devices,) + tops.shape)
     leaving = jnp.concatenate([packed.reshape(devices, ghosts, dwidth), tops], axis=1)
     landed = lax.all_to_all(leaving, axes, split_axis=0, concat_axis=0, tiled=True)
-    arrived = landed[:, :ghosts].reshape(devices * ghosts, dwidth)
-    top_boxes = landed[:, ghosts:, :ewidth].reshape(-1, ewidth)
-    top_hot = top_lists == lax.broadcasted_iota(jnp.int32, (1, top_boxes.shape[0]), 1)
-    top_picked = jnp.dot(top_hot.astype(BF), top_boxes, preferred_element_type=F32).astype(BF)
-
-    dens_pool = jnp.concatenate([densities, arrived.T], axis=1)
+    landed = landed.reshape(devices * span, dwidth)
+    slot = lax.broadcasted_iota(jnp.int32, (devices * span, 1), 0)
+    ghost = lax.broadcasted_iota(jnp.int32, (1, devices * ghosts), 1)
+    wanted = slot == ghost // ghosts * span + ghost % ghosts
+    arrived = dot_t(landed, wanted.astype(BF)).astype(BF)
+    top_at = top_lists // own_tops * span + ghosts + top_lists % own_tops
+    top_hot = top_at == lax.broadcasted_iota(jnp.int32, (1, devices * span), 1)
+    top_picked = jnp.dot(top_hot.astype(BF), landed[:, :ewidth], preferred_element_type=F32)
+    top_picked = top_picked.astype(BF)
+
+    dens_pool = jnp.concatenate([densities, arrived], axis=1)
     mult_pool = jnp.einsum("dl,de->el", dens_pool, p2m, preferred_element_type=F32).astype(BF)
     far, top_far = far_call(
         far_lists,
         m2l_rows,
-        *split(mult_pool),
+        mult_pool,
         top_picked.reshape(offset_count // BLOCK, 1, BLOCK * ewidth),
     )
-    near = near_call(near_lists, p2p_rows, *split(dens_pool), densities)
+    near = near_call(near_lists, p2p_rows, dens_pool, densities)
 
     local_exp = top_far.T.astype(BF)
     leaf_far = None

time: 163 us -> 159 us (0.975)
  other arithmetic: 7.03 us -> 1.88 us
  local copies, waits for them, and re-layouts: 18 us -> 14.3 us
  matrix products: 5.77 us -> 8.95 us
  Pallas kernels: 123 us -> 125 us
    dot_general x1 -> x2, matrix products: 0.91 us -> 4.46 us  [the longest x1 2.27 us: dot_t(): lax.dot_general(left, right, (((0,), (0,)), ((), ())), preferred_element_...]
    another operation x2 -> x0, other arithmetic: 2.9 us -> none
    slice x2 -> x0, local copies, waits for them, and re-layouts: 2.83 us -> none  [the longest x1 1.9 us: shards(): arrived = landed[:, :ghosts].reshape(devices * ghosts, dwidth)]
    concatenate x2 -> x1, other arithmetic: 2.9 us -> 0.88 us  [shards(): dens_pool = jnp.concatenate([densities, arrived], axis=1)]
    reshape x1 -> x0, local copies, waits for them, and re-layouts: 1.98 us -> none  [shards(): arrived = landed[:, :ghosts].reshape(devices * ghosts, dwidth)]
    unnamed x36 -> x34, local copies, waits for them, and re-layouts: 3.57 us -> 4.73 us
where the time goes in v4:
time: 159 us; the launch traced here: 158 us
  Pallas kernels  125 us (79%)
  local copies, waits for them, and re-layouts  14.3 us (9%)
  matrix products  8.95 us (6%)
  starting transfers between devices  7.41 us (5%)
  other arithmetic  1.88 us (1%)
    pallas_call x1, Pallas kernels, far_call(): pl.pallas_call(far_kernel, grid=(offsets // BLOCK,), in_specs=[pl.BlockSp...  87.9 us
    pallas_call x4, Pallas kernels, as_rows(): pl.pallas_call(functools.partial(rows_kernel, width, period, lanes), grid...  23.7 us
    pallas_call x1, Pallas kernels, near_call(): pl.pallas_call(near_kernel, out_shape=jax.ShapeDtypeStruct((dwidth, leave...  13.7 us
    all_to_all x1, starting transfers between devices, shards(): lax.all_to_all(leaving, axes, split_axis=0, concat_axis=0, tiled=True)  7.41 us
    unnamed x34, local copies, waits for them, and re-layouts  4.73 us
  transfers between devices with their start and end apart: 1, of which 0 were waited for; matrix products, arithmetic and copies ran while one was open for 1% of the time, Pallas kernels for 14%

profile of v4, /device:TPU:0, one launch (start us, length us, event | category | flops | bytes accessed | tf_op | source)
XLA Modules:
  0.0 158.1 jit_solution(4369040917725279303)
XLA Ops:
  0.0 1.1 copy-done.5
  1.1 0.9 shard_map.110
  2.0 1.1 reshape.121
  3.1 0.6 copy-done.12
  3.7 0.2 convolution_convert_fusion.1
  4.1 0.3 fusion.9
  4.4 0.2 fusion.11
  4.6 0.3 fusion.19
  4.9 0.7 fusion.4
  5.9 1.0 pad_maximum_fusion
  6.9 7.4 %all-to-all-start = ((bf16[32,40,192]{2,1,0:T(8,128)(2,1)}), bf16[32,40,192]{2,1,0:T(8,128)(2,1)}, u32[]{:S(2)}, u32[]{:S(2)}) async-start(bf16[32,40,192]{2,1,0:T(8,128)(2,1)} %pad_maximum_fusion), calls=%async_computation | async-start | bytes 1310720 | tf_op jit(solution)/shard_map/all_to_all | solution.py:197
  14.3 20.4 %shard_map.112.m2l = bf16[33600,168]{1,0:T(8,128)(2,1)} custom-call(bf16[44100,128]{1,0:T(8,128)(2,1)} %bitcast.87), custom_call_target="tpu_custom_call" | custom-call | tf_op jit(solution)/shard_map/pallas_call | solution.py:72
  34.7 0.9 shard_map.114
  35.6 1.5 shard_map.109.p2p
  37.2 1.6 %reshape.132 = bf16[168,192]{1,0:T(8,128)(2,1)} reshape(bf16[32256]{0:T(1024)(128)(2,1)} %param.20) | data formatting | bytes 129024 | tf_op jit(solution)/shard_map/reshape | solution.py:179
  38.8 2.3 %fusion.5 = bf16[192,1024]{1,0:T(8,128)(2,1)S(1)} fusion(bf16[1280,192]{1,0:T(8,128)(2,1)} %bitcast.12, s32[1024]{0:T(1024)S(1)} %fusion.28), kind=kOutput, calls=%fused_computation.8 | convolution fusion | flops 504823808 | bytes 888832 | tf_op jit(solution)/shard_map/dot_general | solution.py:36
  41.1 1.1 fusion.2.pool
  42.2 0.9 pad_maximum_fusion.1.pool
  43.1 2.2 %convolution_convert_fusion.2 = bf16[200,168]{0,1:T(8,128)(2,1)} fusion(bf16[1280,192]{1,0:T(8,128)(2,1)} %bitcast.12, s32[200]{0:T(256)S(1)} %bitcast.92), kind=kOutput, calls=%fused_computation.13 | convolution fusion | flops 86305600 | bytes 559520 | tf_op jit(solution)/shard_map/dot_general | solution.py:205
  45.3 1.6 %copy.18 = bf16[200,168]{1,0:T(8,128)(2,1)} copy(bf16[200,168]{0,1:T(8,128)(2,1)} %convolution_convert_fusion.2) | data formatting | bytes 134400 | tf_op jit(solution)/shard_map/convert_element_type | solution.py:206
  46.9 1.8 %reshape.141.top = bf16[25,1,1344]{2,1,0:T(2,128)(2,1)} reshape(bf16[200,168]{1,0:T(8,128)(2,1)} %copy.18) | data formatting | bytes 134400 | tf_op jit(solution)/shard_map/reshape | solution.py:214
  48.7 0.9 copy-done.3
  49.6 1.0 copy-done.4
  50.7 1.0 copy-done.7
  51.7 87.9 %shard_map.113 = (f32[168,512]{1,0:T(8,128)S(1)}, f32[1,168]{1,0:T(1,128)S(1)}) custom-call(s32[200,512]{1,0:T(8,128)S(1)} %copy-done.7, bf16[33600,168]{1,0:T(8,128)(2,1)} %shard_map.112.m2l, bf16[168,1536]{1,0:T(8,128)(2,1)S(1)} %copy-done.4, bf16[25,1,1344]{2,1,0:T(2,128)(2,1)S(1)} %copy-done.3), custom_call_target="tpu_custom_call" | custom-call | tf_op jit(solution)/shard_map/pallas_call | solution.py:110
  139.6 0.2 fusion.32
  139.8 0.2 fusion.8
  140.0 0.3 convolution_bitcast_fusion
  140.3 1.1 copy.41
  141.4 1.9 %copy.22 = f32[168,512]{1,0:T(8,128)} copy(f32[168,512]{0,1:T(8,128)} %bitcast.89) | data formatting | bytes 688128 | tf_op jit(solution)/shard_map/reshape | solution.py:223
  143.4 13.7 %shard_map.111 = f32[192,512]{1,0:T(8,128)S(1)} custom-call(s32[26,512]{1,0:T(8,128)S(1)} %copy-done.10, bf16[5184,192]{1,0:T(8,128)(2,1)S(1)} %shard_map.109.p2p, bf16[192,1536]{1,0:T(8,128)(2,1)S(1)} %copy-done, bf16[192,512]{1,0:T(8,128)(2,1)S(1)} %copy-done.2), custom_call_target="tpu_custom_call" | custom-call | tf_op jit(solution)/shard_map/pallas_call | solution.py:148
  157.1 1.0 fusion.6
  (38 shorter events, 0.5 us)
Async XLA Ops:
  0.0 3.7 %copy-start.2 = (bf16[192,512]{1,0:T(8,128)(2,1)S(1)}, bf16[192,512]{1,0:T(8,128)(2,1)}, u32[]{:S(2)}) copy-start(bf16[192,512]{1,0:T(8,128)(2,1)} %own.1) | copy-start | bytes 589828
  0.0 1.1 copy-start.5
  3.1 0.6 copy-start.12
  4.1 0.8 copy-start.16
  6.9 31.9 %all-to-all-start = ((bf16[32,40,192]{2,1,0:T(8,128)(2,1)}), bf16[32,40,192]{2,1,0:T(8,128)(2,1)}, u32[]{:S(2)}, u32[]{:S(2)}) async-start(bf16[32,40,192]{2,1,0:T(8,128)(2,1)} %pad_maximum_fusion), calls=%async_computation | async-start | bytes 1310720 | tf_op jit(solution)/shard_map/all_to_all | solution.py:197
  14.3 20.4 %copy-start.6 = (bf16[225792]{0:T(1024)(128)(2,1)S(1)}, bf16[225792]{0:T(1024)(128)(2,1)}, u32[]{:S(2)}) copy-start(bf16[225792]{0:T(1024)(128)(2,1)} %param.19) | copy-start | bytes 1354756
  14.3 21.3 %copy-start.1 = (bf16[995328]{0:T(1024)(128)(2,1)S(1)}, bf16[995328]{0:T(1024)(128)(2,1)}, u32[]{:S(2)}) copy-start(bf16[995328]{0:T(1024)(128)(2,1)} %param.21) | copy-start | bytes 5971972
  35.6 3.2 %copy-start.15 = (s32[200,1]{0,1:T(1,128)S(1)}, s32[200,1]{0,1:T(1,128)}, u32[]{:S(2)}) copy-start(s32[200,1]{0,1:T(1,128)} %param.15) | copy-start | bytes 2404
  38.8 2.3 %copy-start.13 = (bf16[192,168]{1,0:T(8,128)(2,1)S(1)}, bf16[192,168]{1,0:T(8,128)(2,1)}, u32[]{:S(2)}) copy-start(bf16[192,168]{1,0:T(8,128)(2,1)} %copy-done.12) | copy-start | bytes 193540
  48.7 0.9 copy-start.3
  49.6 1.0 copy-start.4
  50.7 1.0 copy-start.7
  139.5 0.7 copy-start.8
  140.3 3.1 %copy-start = (bf16[192,1536]{1,0:T(8,128)(2,1)S(1)}, bf16[192,1536]{1,0:T(8,128)(2,1)}, u32[]{:S(2)}) copy-start(bf16[192,1536]{1,0:T(8,128)(2,1)} %pad_maximum_fusion.1.pool) | copy-start | bytes 1769476
  140.3 3.1 %copy-start.10 = (s32[26,512]{1,0:T(8,128)S(1)}, s32[26,512]{1,0:T(8,128)}, u32[]{:S(2)}) copy-start(s32[26,512]{1,0:T(8,128)} %lists.2) | copy-start | bytes 159748
  143.3 13.7 %copy-start.9 = (f32[168,512]{1,0:T(8,128)S(1)}, f32[168,512]{1,0:T(8,128)}, u32[]{:S(2)}) copy-start(f32[168,512]{1,0:T(8,128)} %copy-done.8) | copy-start | bytes 1032196
  143.3 13.8 %copy-start.11 = (f32[168,512]{1,0:T(8,128)S(1)}, f32[168,512]{1,0:T(8,128)}, u32[]{:S(2)}) copy-start(f32[168,512]{1,0:T(8,128)} %copy.22) | copy-start | bytes 1032196
  143.3 13.8 %copy-start.14 = (bf16[168,192]{1,0:T(8,128)(2,1)S(1)}, bf16[168,192]{1,0:T(8,128)(2,1)}, u32[]{:S(2)}) copy-start(bf16[168,192]{1,0:T(8,128)(2,1)} %reshape.132) | copy-start | bytes 193540

commit v5 on v4

--- a/solution.py
+++ b/solution.py
@@ -9,7 +9,7 @@
 from jax.sharding import PartitionSpec as P
 
 LEVELS = 3
-BLOCK = 8
+BLOCK = 40
 BF = jnp.bfloat16
 F32 = jnp.float32
 
@@ -29,7 +29,11 @@
 
 
 def pick(pool, row):
-    return jnp.dot(pool[...], one_hot(row, pool.shape[1]), preferred_element_type=F32)
+    parts = []
+    for at in range(0, row.shape[1], 256):
+        hot = one_hot(row[:, at : at + 256], pool.shape[1])
+        parts.append(jnp.dot(pool[...], hot, preferred_element_type=F32))
+    return jnp.concatenate(parts, axis=1)
 
 
 def dot_t(left, right):
@@ -99,7 +103,8 @@
         start = pl.multiple_of(pair * (2 * ewidth), 16)
         picked[pl.ds(start, 2 * ewidth), :] = jnp.concatenate(both, axis=0).astype(BF)
 
-    far[...] += dot_t(m2l[...], picked[...])
+    for at in range(0, far.shape[1], 256):
+        far[:, at : at + 256] += dot_t(m2l[...], picked[:, at : at + 256])
     top_far[...] += jnp.dot(top[0], m2l[...], preferred_element_type=F32)
 
 
@@ -139,7 +144,8 @@
         picked[pl.ds(pl.multiple_of(c * dwidth, 16), dwidth), :] = found
 
     picked[classes * dwidth :, :] = own[...]
-    out[...] = dot_t(p2p[...], picked[...])
+    for at in range(0, leaves, 256):
+        out[:, at : at + 256] = dot_t(p2p[...], picked[:, at : at + 256])
 
 
 def near_call(near_lists, p2p_rows, pool, own):

time: 159 us -> 159 us (level)
  no operation moved by 1% of the time
where the time goes in v5:
time: 159 us; the launch traced here: 158 us
  Pallas kernels  126 us (79%)
  local copies, waits for them, and re-layouts  14.4 us (9%)
  matrix products  8.95 us (6%)
  starting transfers between devices  7.41 us (5%)
  other arithmetic  1.88 us (1%)
    pallas_call x1, Pallas kernels, far_call(): pl.pallas_call(far_kernel, grid=(offsets // BLOCK,), in_specs=[pl.BlockSp...  87.7 us
    pallas_call x4, Pallas kernels, as_rows(): pl.pallas_call(functools.partial(rows_kernel, width, period, lanes), grid...  23.7 us
    pallas_call x1, Pallas kernels, near_call(): pl.pallas_call(near_kernel, out_shape=jax.ShapeDtypeStruct((dwidth, leave...  14.2 us
    all_to_all x1, starting transfers between devices, shards(): lax.all_to_all(leaving, axes, split_axis=0, concat_axis=0, tiled=True)  7.41 us
    unnamed x34, local copies, waits for them, and re-layouts  4.73 us
  transfers between devices with their start and end apart: 1, of which 0 were waited for; matrix products, arithmetic and copies ran while one was open for 1% of the time, Pallas kernels for 14%

profile of v5, /device:TPU:0, one launch (start us, length us, event | category | flops | bytes accessed | tf_op | source)
XLA Modules:
  0.0 158.4 jit_solution(6619258985219767220)
XLA Ops:
  0.0 1.1 copy-done.5
  1.1 0.9 shard_map.110
  2.0 1.1 reshape.121
  3.1 0.6 copy-done.12
  3.7 0.2 convolution_convert_fusion.1
  4.1 0.3 fusion.9
  4.4 0.2 fusion.11
  4.6 0.3 fusion.19
  4.9 0.7 fusion.4
  5.9 1.0 pad_maximum_fusion
  6.9 7.4 %all-to-all-start = ((bf16[32,40,192]{2,1,0:T(8,128)(2,1)}), bf16[32,40,192]{2,1,0:T(8,128)(2,1)}, u32[]{:S(2)}, u32[]{:S(2)}) async-start(bf16[32,40,192]{2,1,0:T(8,128)(2,1)} %pad_maximum_fusion), calls=%async_computation | async-start | bytes 1310720 | tf_op jit(solution)/shard_map/all_to_all | solution.py:203
  14.3 20.4 %shard_map.112.m2l = bf16[33600,168]{1,0:T(8,128)(2,1)} custom-call(bf16[44100,128]{1,0:T(8,128)(2,1)} %bitcast.87), custom_call_target="tpu_custom_call" | custom-call | tf_op jit(solution)/shard_map/pallas_call | solution.py:76
  34.7 0.9 shard_map.114
  35.6 1.5 shard_map.109.p2p
  37.2 1.6 %reshape.132 = bf16[168,192]{1,0:T(8,128)(2,1)} reshape(bf16[32256]{0:T(1024)(128)(2,1)} %param.20) | data formatting | bytes 129024 | tf_op jit(solution)/shard_map/reshape | solution.py:185
  38.8 2.3 %fusion.5 = bf16[192,1024]{1,0:T(8,128)(2,1)S(1)} fusion(bf16[1280,192]{1,0:T(8,128)(2,1)} %bitcast.12, s32[1024]{0:T(1024)S(1)} %fusion.28), kind=kOutput, calls=%fused_computation.8 | convolution fusion | flops 504823808 | bytes 888832 | tf_op jit(solution)/shard_map/dot_general | solution.py:40
  41.1 1.1 fusion.2.pool
  42.2 0.9 pad_maximum_fusion.1.pool
  43.1 2.2 %convolution_convert_fusion.2 = bf16[200,168]{0,1:T(8,128)(2,1)} fusion(bf16[1280,192]{1,0:T(8,128)(2,1)} %bitcast.12, s32[200]{0:T(256)S(1)} %bitcast.92), kind=kOutput, calls=%fused_computation.13 | convolution fusion | flops 86305600 | bytes 559520 | tf_op jit(solution)/shard_map/dot_general | solution.py:211
  45.3 1.6 %copy.18 = bf16[200,168]{1,0:T(8,128)(2,1)} copy(bf16[200,168]{0,1:T(8,128)(2,1)} %convolution_convert_fusion.2) | data formatting | bytes 134400 | tf_op jit(solution)/shard_map/convert_element_type | solution.py:212
  46.9 1.9 %reshape.141.top = bf16[5,1,6720]{2,1,0:T(2,128)(2,1)} reshape(bf16[200,168]{1,0:T(8,128)(2,1)} %copy.18) | data formatting | bytes 134400 | tf_op jit(solution)/shard_map/reshape | solution.py:220
  48.8 0.9 copy-done.3
  49.7 1.0 copy-done.4
  50.7 1.0 copy-done.7
  51.7 87.7 %shard_map.113 = (f32[168,512]{1,0:T(8,128)S(1)}, f32[1,168]{1,0:T(1,128)S(1)}) custom-call(s32[200,512]{1,0:T(8,128)S(1)} %copy-done.7, bf16[33600,168]{1,0:T(8,128)(2,1)} %shard_map.112.m2l, bf16[168,1536]{1,0:T(8,128)(2,1)S(1)} %copy-done.4, bf16[5,1,6720]{2,1,0:T(2,128)(2,1)S(1)} %copy-done.3), custom_call_target="tpu_custom_call" | custom-call | tf_op jit(solution)/shard_map/pallas_call | solution.py:115
  139.4 0.2 fusion.32
  139.6 0.2 fusion.8
  139.8 0.3 convolution_bitcast_fusion
  140.1 1.1 copy.41
  141.2 1.9 %copy.22 = f32[168,512]{1,0:T(8,128)} copy(f32[168,512]{0,1:T(8,128)} %bitcast.89) | data formatting | bytes 688128 | tf_op jit(solution)/shard_map/reshape | solution.py:229
  143.2 14.2 %shard_map.111 = f32[192,512]{1,0:T(8,128)S(1)} custom-call(s32[26,512]{1,0:T(8,128)S(1)} %copy-done.10, bf16[5184,192]{1,0:T(8,128)(2,1)S(1)} %shard_map.109.p2p, bf16[192,1536]{1,0:T(8,128)(2,1)S(1)} %copy-done, bf16[192,512]{1,0:T(8,128)(2,1)S(1)} %copy-done.2), custom_call_target="tpu_custom_call" | custom-call | tf_op jit(solution)/shard_map/pallas_call | solution.py:154
  157.4 1.0 fusion.6
  (38 shorter events, 0.5 us)
Async XLA Ops:
  0.0 3.7 %copy-start.2 = (bf16[192,512]{1,0:T(8,128)(2,1)S(1)}, bf16[192,512]{1,0:T(8,128)(2,1)}, u32[]{:S(2)}) copy-start(bf16[192,512]{1,0:T(8,128)(2,1)} %own.1) | copy-start | bytes 589828
  0.0 1.1 copy-start.5
  3.1 0.6 copy-start.12
  4.1 0.8 copy-start.16
  6.9 31.9 %all-to-all-start = ((bf16[32,40,192]{2,1,0:T(8,128)(2,1)}), bf16[32,40,192]{2,1,0:T(8,128)(2,1)}, u32[]{:S(2)}, u32[]{:S(2)}) async-start(bf16[32,40,192]{2,1,0:T(8,128)(2,1)} %pad_maximum_fusion), calls=%async_computation | async-start | bytes 1310720 | tf_op jit(solution)/shard_map/all_to_all | solution.py:203
  14.3 20.4 %copy-start.6 = (bf16[225792]{0:T(1024)(128)(2,1)S(1)}, bf16[225792]{0:T(1024)(128)(2,1)}, u32[]{:S(2)}) copy-start(bf16[225792]{0:T(1024)(128)(2,1)} %param.19) | copy-start | bytes 1354756
  14.3 21.3 %copy-start.1 = (bf16[995328]{0:T(1024)(128)(2,1)S(1)}, bf16[995328]{0:T(1024)(128)(2,1)}, u32[]{:S(2)}) copy-start(bf16[995328]{0:T(1024)(128)(2,1)} %param.21) | copy-start | bytes 5971972
  35.6 3.2 %copy-start.15 = (s32[200,1]{0,1:T(1,128)S(1)}, s32[200,1]{0,1:T(1,128)}, u32[]{:S(2)}) copy-start(s32[200,1]{0,1:T(1,128)} %param.15) | copy-start | bytes 2404
  38.8 2.3 %copy-start.13 = (bf16[192,168]{1,0:T(8,128)(2,1)S(1)}, bf16[192,168]{1,0:T(8,128)(2,1)}, u32[]{:S(2)}) copy-start(bf16[192,168]{1,0:T(8,128)(2,1)} %copy-done.12) | copy-start | bytes 193540
  48.8 0.9 copy-start.3
  49.7 1.0 copy-start.4
  50.7 1.0 copy-start.7
  139.4 0.7 copy-start.8
  140.1 3.1 %copy-start = (bf16[192,1536]{1,0:T(8,128)(2,1)S(1)}, bf16[192,1536]{1,0:T(8,128)(2,1)}, u32[]{:S(2)}) copy-start(bf16[192,1536]{1,0:T(8,128)(2,1)} %pad_maximum_fusion.1.pool) | copy-start | bytes 1769476
  140.1 3.1 %copy-start.10 = (s32[26,512]{1,0:T(8,128)S(1)}, s32[26,512]{1,0:T(8,128)}, u32[]{:S(2)}) copy-start(s32[26,512]{1,0:T(8,128)} %lists.2) | copy-start | bytes 159748
  143.2 14.2 %copy-start.9 = (f32[168,512]{1,0:T(8,128)S(1)}, f32[168,512]{1,0:T(8,128)}, u32[]{:S(2)}) copy-start(f32[168,512]{1,0:T(8,128)} %copy-done.8) | copy-start | bytes 1032196
  143.2 14.2 %copy-start.11 = (f32[168,512]{1,0:T(8,128)S(1)}, f32[168,512]{1,0:T(8,128)}, u32[]{:S(2)}) copy-start(f32[168,512]{1,0:T(8,128)} %copy.22) | copy-start | bytes 1032196
  143.2 14.2 %copy-start.14 = (bf16[168,192]{1,0:T(8,128)(2,1)S(1)}, bf16[168,192]{1,0:T(8,128)(2,1)}, u32[]{:S(2)}) copy-start(bf16[168,192]{1,0:T(8,128)(2,1)} %reshape.132) | copy-start | bytes 193540
